TPU v7x, 32 devices: a whole 2x2x4 slice. The times are simulated.
32 devices in a mesh: row: 4 (over z), col: 2 (over y), seq: 4 (over x, core).
Axes of the slice: x: 2, y: 2, z: 4, core: 2. Of those that a mesh axis runs over, the one named last changes fastest.
Arguments:
- motion_ids: int32 [384], P('col'), may hold values from 0 to 511
- audio_ids: int32 [384], P('col'), may hold values from 0 to 1023
- segment_ids: int32 [384], replicated, may hold values from 0 to 3, never falling along the last dimension, each value on 1 to 192 neighbouring positions
- motion_table: bfloat16 [512, 8192], P(None, ('row', 'seq')), may hold values from -40 to 40
- audio_table: bfloat16 [1024, 8192], P(None, ('row', 'seq')), may hold values from -40 to 40
- norm_gain: float32 [8192], P(('row', 'seq')), may hold values from 0.5 to 1.5
- w_query: bfloat16 [8192, 8192], P(('row', 'seq'), 'col'), may hold values from -0.1875 to 0.1875
- w_key: bfloat16 [8192, 1024], P(('row', 'seq'), 'col'), may hold values from -0.0625 to 0.0625
- w_value: bfloat16 [8192, 1024], P(('row', 'seq'), 'col'), may hold values from -0.0625 to 0.0625
- w_out: bfloat16 [8192, 8192], P('col', ('row', 'seq')), may hold values from -0.0625 to 0.0625
- out_grad: bfloat16 [384, 8192], P('col', ('row', 'seq')), may hold values from -6 to 6
Outputs:
- layer_out: bfloat16 [384, 8192], P('col', ('row', 'seq'))
- grad_input: bfloat16 [384, 8192], P('col', ('row', 'seq'))
- grad_gain: float32 [8192], P(('row', 'seq'))
- grad_wq: float32 [8192, 8192], P(('row', 'seq'), 'col')
- grad_wk: float32 [8192, 1024], P(('row', 'seq'), 'col')
- grad_wv: float32 [8192, 1024], P(('row', 'seq'), 'col')
- grad_wo: float32 [8192, 8192], P('col', ('row', 'seq'))
Inputs may be any that keep to these rules, and one draw needn't show every extreme that they name: `segment_ids`: document ids never fall along the sequence; no document is longer than 192 positions, and one is exactly that long.
All inputs are finite; a program needn't handle non-finite values.
Results may differ from a plain program's by a relative error of at most 0.023.
Values may be sent and summed in bfloat16 or wider, within the bound.
A program may use at most 128 MiB of HBM per device.

v0:
```python
import jax
import jax.numpy as jnp
from jax import lax
from jax.sharding import PartitionSpec as P

D = 8192
H = 64
KV = 8
HD = 128


epsilon = 1e-05
softcap = 20.0
rope_base = 500000.0


def rotary_tables(positions, head_size):
    half_size = head_size // 2
    frequency = rope_base ** (-(jnp.arange(half_size, dtype=jnp.float32) * 2.0) / head_size)
    angles = positions.astype(jnp.float32)[:, None] * frequency[None, :]
    return (jnp.cos(angles), jnp.sin(angles))


def rotate_pairs(values, cosines, sines):
    half_size = values.shape[-1] // 2
    first_half = values[..., :half_size]
    second_half = values[..., half_size:]
    cos_part = cosines[:, None, :]
    sin_part = sines[:, None, :]
    return jnp.concatenate(
        [
            first_half * cos_part - second_half * sin_part,
            second_half * cos_part + first_half * sin_part,
        ],
        axis=-1,
    )


def rotate_back(values, cosines, sines):
    half_size = values.shape[-1] // 2
    first_half = values[..., :half_size]
    second_half = values[..., half_size:]
    cos_part = cosines[:, None, :]
    sin_part = sines[:, None, :]
    return jnp.concatenate(
        [
            first_half * cos_part + second_half * sin_part,
            second_half * cos_part - first_half * sin_part,
        ],
        axis=-1,
    )


def rope_round(values, positions):
    cosines, sines = rotary_tables(positions, HD)
    row_total = values.shape[0]
    return (
        rotate_pairs(values.reshape(row_total, -1, HD), cosines, sines)
        .reshape(row_total, -1)
        .astype(jnp.bfloat16)
    )


def plain_round(values, positions):
    return values.astype(jnp.bfloat16)


def per_device(
    motion_ids,
    audio_ids,
    segment_ids,
    motion_table,
    audio_table,
    norm_gain,
    w_query,
    w_key,
    w_value,
    w_out,
    out_grad,
):
    seq_len = segment_ids.shape[0]
    row_devices = lax.axis_size("row")
    seq_devices = lax.axis_size("seq")
    row_index = lax.axis_index("row")
    seq_index = lax.axis_index("seq")
    col_index = lax.axis_index("col")
    block_len = seq_len // (row_devices * seq_devices)
    quarter_len = seq_len // row_devices
    query_width = w_query.shape[1]
    kv_width = w_key.shape[1]
    heads_col = query_width // HD
    kv_col = kv_width // HD
    group_size = H // KV
    score_scale = HD ** (-0.5)
    block_pos = (row_index * seq_devices + seq_index) * block_len + jnp.arange(
        block_len, dtype=jnp.int32
    )
    embedded = (
        jnp.take(motion_table, motion_ids, axis=0).astype(jnp.float32)
        + jnp.take(audio_table, audio_ids, axis=0).astype(jnp.float32)
    ).astype(jnp.bfloat16)
    residual = embedded.astype(jnp.float32)
    squares = lax.psum(jnp.sum(residual * residual, axis=1), ("row", "seq"))
    inverse = lax.rsqrt(squares / D + epsilon)
    normed = (residual * inverse[:, None] * norm_gain[None, :]).astype(jnp.bfloat16)
    normed_all = lax.all_gather(normed, "col", axis=0, tiled=True)
    query_pos = row_index * quarter_len + jnp.arange(quarter_len, dtype=jnp.int32)
    head_first = col_index * heads_col + seq_index * (heads_col // seq_devices)
    head_count = heads_col // seq_devices

    def to_heads(term, finish):
        own_share = lax.psum_scatter(
            term(jnp.int32(0), block_len * lax.axis_size(("row", "seq"))),
            ("row", "seq"),
            scatter_dimension=0,
            tiled=True,
        )
        return lax.all_to_all(
            finish(own_share, block_pos), "seq", split_axis=1, concat_axis=0, tiled=True
        )

    def to_rows(heads_part):
        own_share = lax.all_to_all(heads_part, "seq", split_axis=0, concat_axis=1, tiled=True)
        return lax.all_gather(own_share, ("row", "seq"), axis=0, tiled=True)

    def query_term(first_row, row_count):
        return jnp.dot(normed_all, w_query, preferred_element_type=jnp.float32)

    queries = to_heads(query_term, rope_round)
    picked = normed_all
    kv_sum = lax.psum_scatter(
        jnp.concatenate(
            [
                jnp.dot(picked, w_key, preferred_element_type=jnp.float32),
                jnp.dot(picked, w_value, preferred_element_type=jnp.float32),
            ],
            axis=1,
        ),
        ("row", "seq"),
        scatter_dimension=0,
        tiled=True,
    )
    kv_block = jnp.concatenate(
        [rope_round(kv_sum[:, :kv_width], block_pos), kv_sum[:, kv_width:].astype(jnp.bfloat16)],
        axis=1,
    )
    kv_all = lax.all_gather(kv_block, ("row", "seq"), axis=0, tiled=True)
    query_len = queries.shape[0]
    kv_slot = (
        head_first + jnp.arange(head_count, dtype=jnp.int32)
    ) // group_size - col_index * kv_col
    key_sel = jnp.take(kv_all[:, :kv_width].reshape(seq_len, kv_col, HD), kv_slot, axis=1)
    value_sel = jnp.take(kv_all[:, kv_width:].reshape(seq_len, kv_col, HD), kv_slot, axis=1)
    key_pos = jnp.arange(seq_len, dtype=jnp.int32)
    allowed = (key_pos[None, :] <= query_pos[:, None]) & (
        segment_ids[None, :] == jnp.take(segment_ids, query_pos)[:, None]
    )
    query_heads = queries.reshape(query_len, head_count, HD)
    raw_scores = (
        jnp.einsum("qhd,khd->hqk", query_heads, key_sel, preferred_element_type=jnp.float32)
        * score_scale
    )
    capped = softcap * jnp.tanh(raw_scores / softcap)
    weights = jnp.where(allowed[None], jnp.exp(capped), 0.0)
    totals = jnp.sum(weights, axis=2)
    attended = jnp.einsum(
        "hqk,khd->qhd", weights.astype(jnp.bfloat16), value_sel, preferred_element_type=jnp.float32
    )
    attn_out = (
        (attended / totals.T[:, :, None]).astype(jnp.bfloat16).reshape(query_len, head_count * HD)
    )
    out_all = to_rows(attn_out)
    picked = out_all
    branch_sum = lax.psum_scatter(
        jnp.dot(picked, w_out, preferred_element_type=jnp.float32).astype(jnp.bfloat16),
        "col",
        scatter_dimension=0,
        tiled=True,
    ).astype(jnp.float32)
    layer_out = (residual + branch_sum).astype(jnp.bfloat16)
    grad_all = lax.all_gather(out_grad, "col", axis=0, tiled=True)
    grad_wo = jnp.einsum("ln,ld->nd", out_all, grad_all, preferred_element_type=jnp.float32)

    def dout_term(first_row, row_count):
        return jnp.einsum("ld,nd->ln", grad_all, w_out, preferred_element_type=jnp.float32)

    out_heads = to_heads(dout_term, plain_round).reshape(query_len, head_count, HD)
    attn_probs = weights / totals[:, :, None]
    prob_grads = jnp.einsum(
        "qhd,khd->hqk", out_heads, value_sel, preferred_element_type=jnp.float32
    )
    row_dots = jnp.sum(attn_probs * prob_grads, axis=2, keepdims=True)
    grad_scores = (
        attn_probs * (prob_grads - row_dots) * (1.0 - (capped / softcap) ** 2) * score_scale
    ).astype(jnp.bfloat16)
    grad_query = jnp.einsum(
        "hqk,khd->qhd", grad_scores, key_sel, preferred_element_type=jnp.float32
    )
    grad_key_heads = jnp.einsum(
        "hqk,qhd->khd", grad_scores, query_heads, preferred_element_type=jnp.float32
    )
    grad_value_heads = jnp.einsum(
        "hqk,qhd->khd",
        attn_probs.astype(jnp.bfloat16),
        out_heads,
        preferred_element_type=jnp.float32,
    )
    slot_mask = (kv_slot[:, None] == jnp.arange(kv_col, dtype=jnp.int32)[None, :]).astype(
        jnp.float32
    )
    grad_key_part = jnp.sum(
        grad_key_heads[:, :, None, :] * slot_mask[None, :, :, None], axis=1
    ).reshape(seq_len, kv_width)
    grad_value_part = jnp.sum(
        grad_value_heads[:, :, None, :] * slot_mask[None, :, :, None], axis=1
    ).reshape(seq_len, kv_width)
    kv_grad_sum = lax.psum_scatter(
        jnp.concatenate([grad_key_part, grad_value_part], axis=1).astype(jnp.bfloat16),
        ("row", "seq"),
        scatter_dimension=0,
        tiled=True,
    ).astype(jnp.float32)
    cos_block, sin_block = rotary_tables(block_pos, HD)
    grad_key_block = (
        rotate_back(kv_grad_sum[:, :kv_width].reshape(block_len, kv_col, HD), cos_block, sin_block)
        .reshape(block_len, kv_width)
        .astype(jnp.bfloat16)
    )
    kv_grad_block = jnp.concatenate(
        [grad_key_block, kv_grad_sum[:, kv_width:].astype(jnp.bfloat16)], axis=1
    )
    kv_grad_all = lax.all_gather(kv_grad_block, ("row", "seq"), axis=0, tiled=True)
    cos_query, sin_query = rotary_tables(query_pos, HD)
    grad_query_round = (
        rotate_back(grad_query, cos_query, sin_query)
        .reshape(query_len, head_count * HD)
        .astype(jnp.bfloat16)
    )
    grad_query_all = to_rows(grad_query_round)
    grad_wq = jnp.einsum(
        "ld,ln->dn", normed_all, grad_query_all, preferred_element_type=jnp.float32
    )
    grad_wk = jnp.einsum(
        "ld,ln->dn", normed_all, kv_grad_all[:, :kv_width], preferred_element_type=jnp.float32
    )
    grad_wv = jnp.einsum(
        "ld,ln->dn", normed_all, kv_grad_all[:, kv_width:], preferred_element_type=jnp.float32
    )
    total_term = jnp.einsum(
        "ln,dn->ld", grad_query_all, w_query, preferred_element_type=jnp.float32
    )
    total_term = total_term + jnp.einsum(
        "ln,dn->ld", kv_grad_all[:, :kv_width], w_key, preferred_element_type=jnp.float32
    )
    grad_normed = lax.psum_scatter(
        (
            total_term
            + jnp.einsum(
                "ln,dn->ld", kv_grad_all[:, kv_width:], w_value, preferred_element_type=jnp.float32
            )
        ).astype(jnp.bfloat16),
        "col",
        scatter_dimension=0,
        tiled=True,
    ).astype(jnp.float32)
    scaled_grad = grad_normed * norm_gain[None, :]
    total_dot = lax.psum(jnp.sum(scaled_grad * residual, axis=1), ("row", "seq"))
    grad_input = (
        out_grad.astype(jnp.float32)
        + inverse[:, None] * scaled_grad
        - residual * (inverse**3 * total_dot / D)[:, None]
    ).astype(jnp.bfloat16)
    grad_gain = lax.psum(jnp.sum(grad_normed * residual * inverse[:, None], axis=0), "col")
    return (layer_out, grad_input, grad_gain, grad_wq, grad_wk, grad_wv, grad_wo)


def solution(mesh):
    placed = (
        P("col"),
        P("col"),
        P(),
        P(None, ("row", "seq")),
        P(None, ("row", "seq")),
        P(("row", "seq")),
        P(("row", "seq"), "col"),
        P(("row", "seq"), "col"),
        P(("row", "seq"), "col"),
        P("col", ("row", "seq")),
        P("col", ("row", "seq")),
    )
    return jax.shard_map(
        per_device,
        mesh=mesh,
        in_specs=placed,
        out_specs=(
            P("col", ("row", "seq")),
            P("col", ("row", "seq")),
            P(("row", "seq")),
            P(("row", "seq"), "col"),
            P(("row", "seq"), "col"),
            P(("row", "seq"), "col"),
            P("col", ("row", "seq")),
        ),
        check_vma=False,
    )
```

profile of v0, /device:TPU:0, one launch (start us, length us, event | category | flops | bytes accessed | tf_op | source)
XLA Modules:
  0.0 536.1 jit_solution(7594540054378134432)
XLA Ops:
  7.2 0.8 compare_select_fusion.1
  9.4 2.2 gather_fusion
  11.6 1.0 gather_fusion.1
  12.9 34.9 %psum.21 = f32[192]{0:T(256)S(1)} all-reduce(f32[192]{0:T(256)S(1)} %get-tuple-element.14), channel_id=1, replica_groups=mesh['row'=4,'col'=2,'seq'=4] {'row','seq'}, use_global_device_ids=true, to_apply=%region_1.2 | all-reduce | flops 192 | bytes 1536 | tf_op jit(solution)/shard_map/psum | solution.py:103
  48.5 6.5 %all_gather.18 = bf16[384,512]{1,0:T(8,128)(2,1)S(1)} all-gather(bf16[192,512]{1,0:T(8,128)(2,1)S(1)} %fusion.38), channel_id=1, replica_groups=mesh['row'=4,'col'=2,'seq'=4] {'col'}, dimensions={0}, use_global_device_ids=true | all-gather | bytes 589824 | tf_op jit(solution)/shard_map/all_gather | solution.py:106
  55.7 1.3 pad_maximum_fusion
  57.1 0.9 copy-done.17
  58.0 6.3 %all_gather.21 = bf16[384,512]{1,0:T(8,128)(2,1)S(1)} all-gather(bf16[192,512]{1,0:T(8,128)(2,1)S(1)} %copy-done.17), channel_id=1, replica_groups=mesh['row'=4,'col'=2,'seq'=4] {'col'}, dimensions={0}, use_global_device_ids=true | all-gather | bytes 589824 | tf_op jit(solution)/shard_map/all_gather | solution.py:181
  64.3 0.8 copy-done.4
  65.1 6.9 %fusion.81 = f32[384,4096]{1,0:T(8,128)} fusion(bf16[384,512]{1,0:T(8,128)(2,1)S(1)} %all_gather.21, bf16[4096,512]{1,0:T(8,128)(2,1)} %param.22), kind=kOutput, calls=%fused_computation.152 | convolution fusion | flops 1610612736 | bytes 10878976 | tf_op jit(solution)/shard_map/ld,nd->ln/dot_general | solution.py:185
  72.0 6.8 %fusion.80 = f32[384,4096]{1,0:T(8,128)} fusion(bf16[384,512]{1,0:T(8,128)(2,1)S(1)} %all_gather.18, bf16[512,4096]{1,0:T(8,128)(2,1)} %param.19), kind=kOutput, calls=%fused_computation.151 | convolution fusion | flops 1610612736 | bytes 10878976 | tf_op jit(solution)/shard_map/dot_general | solution.py:127
  79.5 1.3 gather_fusion.2
  81.8 32.3 %reduce-scatter.7.cloned.1.call-done = f32[24,1024]{1,0:T(8,128)} async-done(((f32[384,1024]{1,0:T(8,128)}), f32[24,1024]{1,0:T(8,128)}) %reduce-scatter.7.cloned.1.call-update) | async-done | bytes 98320 | tf_op jit(solution)/shard_map/reduce_scatter | solution.py:131
  114.1 0.8 slice.81
  115.1 0.8 slice.123
  115.9 21.5 %all_gather.19 = bf16[384,1024]{1,0:T(8,128)(2,1)S(1)} all-gather(bf16[24,1024]{1,0:T(8,128)(2,1)S(1)} %pad_maximum_fusion.4), channel_id=1, replica_groups=mesh['row'=4,'col'=2,'seq'=4] {'row','seq'}, dimensions={0}, use_global_device_ids=true | all-gather | bytes 835584 | tf_op jit(solution)/shard_map/all_gather | solution.py:147
  137.5 65.9 %reduce-scatter.13.cloned.1.call-done = f32[24,4096]{1,0:T(8,128)} async-done(((f32[384,4096]{1,0:T(8,128)}), f32[24,4096]{1,0:T(8,128)}) %reduce-scatter.13.cloned.1.call-update) | async-done | bytes 393232 | tf_op jit(solution)/shard_map/reduce_scatter | solution.py:112
  203.4 1.0 convert_element_type.110
  205.1 3.4 all-to-all-start.2
  208.4 83.8 %reduce-scatter.9.cloned.1.call-done = f32[24,4096]{1,0:T(8,128)} async-done(((f32[384,4096]{1,0:T(8,128)}), f32[24,4096]{1,0:T(8,128)}) %reduce-scatter.9.cloned.1.call-update) | async-done | bytes 393232 | tf_op jit(solution)/shard_map/reduce_scatter | solution.py:112
  292.3 1.1 copy.80
  294.5 3.4 all-to-all-start
  299.8 3.4 all-to-all-done
  303.2 1.6 fusion.17
  305.5 1.7 convolution_bitcast_fusion
  307.2 5.9 %convolution_bitcast_fusion.1 = f32[384,8,128]{0,2,1:T(8,128)S(1)} fusion(f32[8,96,384]{2,1,0:T(8,128)} %fusion.17, f32[8,96,384]{2,1,0:T(8,128)S(1)} %get-tuple-element.35, bf16[96,8,128]{2,1,0:T(8,128)(2,1)S(1)} %bitcast.111, f32[8,96]{1,0:T(8,128)S(1)} %get-tuple-element.34, pred[96,384]{1,0:T(8,128)(4,1)} %copy-done.21), kind=kOutput, calls=%fused_computation.10 | convolution fusion | flops 79627392 | bytes 4168704 | tf_op jit(solution)/shard_map/hqk,qhd->khd/dot_general | solution.py:199
  313.6 2.0 copy.74
  315.7 4.7 multiply_reduce_fusion.1
  320.6 1.0 pad_maximum_fusion.1
  322.3 5.9 %convolution_bitcast_fusion.2 = f32[96,8,128]{2,0,1:T(8,128)S(1)} fusion(f32[8,96,384]{2,1,0:T(8,128)} %fusion.17, f32[8,96,384]{2,1,0:T(8,128)S(1)} %copy-done.37, bf16[8,384,128]{2,1,0:T(8,128)(2,1)S(1)} %copy-done.16, pred[8]{0:T(512)(128)(4,1)S(1)} %copy-done.33, f32[8,96]{1,0:T(8,128)S(1)} %copy-done.35, pred[96,384]{1,0:T(8,128)(4,1)S(1)} %copy-done.22), kind=kOutput, calls=%fused_computation.22 | convolution fusion | flops 80020608 | bytes 3578888 | tf_op jit(solution)/shard_map/hqk,khd->qhd/dot_general | solution.py:196
  328.7 7.7 %all_to_all.64 = bf16[4,24,1024]{2,1,0:T(8,128)(2,1)S(1)} all-to-all(bf16[4,24,1024]{2,1,0:T(8,128)(2,1)S(1)} %convert_element_type.113), channel_id=1, replica_groups=mesh['row'=4,'col'=2,'seq'=4] {'seq'}, dimensions={0} | all-to-all | bytes 393216 | tf_op jit(solution)/shard_map/all_to_all | solution.py:123
  337.9 7.7 %all_to_all.65 = bf16[4,24,1024]{2,1,0:T(8,128)(2,1)S(1)} all-to-all(bf16[4,24,1024]{2,1,0:T(8,128)(2,1)S(1)} %all_to_all.50), channel_id=1, replica_groups=mesh['row'=4,'col'=2,'seq'=4] {'seq'}, dimensions={0} | all-to-all | bytes 393216 | tf_op jit(solution)/shard_map/all_to_all | solution.py:123
  346.4 30.2 %reduce-scatter.15.cloned.1.call-done = bf16[24,1024]{1,0:T(8,128)(2,1)} async-done(((bf16[384,1024]{1,0:T(8,128)(2,1)}), bf16[24,1024]{1,0:T(8,128)(2,1)}) %reduce-scatter.15.cloned.1.call-update) | async-done | bytes 49168 | tf_op jit(solution)/shard_map/reduce_scatter | solution.py:217
  376.5 0.8 slice_convert_fusion.1
  377.6 22.0 %all_gather.23 = bf16[384,1024]{1,0:T(8,128)(2,1)S(1)} all-gather(bf16[24,1024]{1,0:T(8,128)(2,1)S(1)} %pad_maximum_fusion.5), channel_id=1, replica_groups=mesh['row'=4,'col'=2,'seq'=4] {'row','seq'}, dimensions={0}, use_global_device_ids=true | all-gather | bytes 835584 | tf_op jit(solution)/shard_map/all_gather | solution.py:232
  399.6 1.4 fusion.46
  401.0 23.7 %all-gather.5.cloned.1.call-done = bf16[384,4096]{1,0:T(8,128)(2,1)} async-done(((bf16[24,4096]{1,0:T(8,128)(2,1)}), bf16[384,4096]{1,0:T(8,128)(2,1)}) %all-gather.5.cloned.1.call-update) | async-done | bytes 3145744 | tf_op jit(solution)/shard_map/all_gather | solution.py:124
  424.7 5.0 fusion.82
  430.7 1.2 fusion.7
  432.2 1.4 fusion.43
  433.6 38.0 %all-gather.3.cloned.1.call-done = bf16[384,4096]{1,0:T(8,128)(2,1)} async-done(((bf16[24,4096]{1,0:T(8,128)(2,1)}), bf16[384,4096]{1,0:T(8,128)(2,1)}) %all-gather.3.cloned.1.call-update) | async-done | bytes 3145744 | tf_op jit(solution)/shard_map/all_gather | solution.py:124
  471.6 5.8 %convolution_convert_fusion = bf16[384,512]{1,0:T(8,128)(2,1)} fusion(bf16[384,4096]{1,0:T(8,128)(2,1)} %all-gather.3.cloned.1.call-done, bf16[4096,512]{1,0:T(8,128)(2,1)} %param.22), kind=kOutput, calls=%fused_computation.21 | convolution fusion | flops 1610809344 | bytes 7733248 | tf_op jit(solution)/shard_map/dot_general | solution.py:175
  477.5 5.8 %fusion.83 = f32[512,4096]{1,0:T(8,128)} fusion(bf16[384,512]{1,0:T(8,128)(2,1)S(1)} %all_gather.18, bf16[384,4096]{1,0:T(8,128)(2,1)S(1)} %copy-done.10), kind=kOutput, calls=%fused_computation.154 | convolution fusion | flops 1610612736 | bytes 11927552 | tf_op jit(solution)/shard_map/ld,ln->dn/dot_general | solution.py:240
  483.4 5.8 %fusion.84 = f32[4096,512]{1,0:T(8,128)} fusion(bf16[384,4096]{1,0:T(8,128)(2,1)S(1)} %copy-done.3, bf16[384,512]{1,0:T(8,128)(2,1)S(1)} %copy-done.5), kind=kOutput, calls=%fused_computation.155 | convolution fusion | flops 1610612736 | bytes 11927552 | tf_op jit(solution)/shard_map/ln,ld->nd/dot_general | solution.py:182
  489.2 1.1 fusion.42
  490.3 31.5 %psum.22 = f32[192]{0:T(256)S(1)} all-reduce(f32[192]{0:T(256)S(1)} %get-tuple-element.9), channel_id=1, replica_groups=mesh['row'=4,'col'=2,'seq'=4] {'row','seq'}, use_global_device_ids=true, to_apply=%region_13.15 | all-reduce | flops 192 | bytes 1536 | tf_op jit(solution)/shard_map/psum | solution.py:267
  521.8 5.5 %psum.23 = f32[512]{0:T(512)} all-reduce(f32[512]{0:T(512)S(1)} %get-tuple-element.8), channel_id=1, replica_groups=mesh['row'=4,'col'=2,'seq'=4] {'col'}, use_global_device_ids=true, to_apply=%region_15.17 | all-reduce | flops 512 | bytes 4096 | tf_op jit(solution)/shard_map/psum | solution.py:273
  527.3 2.0 fusion.35
  (152 shorter events, 15.2 us)
Async XLA Ops:
  7.2 4.4 copy-start
  7.2 106.9 %reduce-scatter.7.cloned.1.call-start = ((), (), s32[]{:S(2)}) async-start(), calls=%async_computation.10 | async-start | bytes 1671168 | tf_op jit(solution)/shard_map/reduce_scatter | solution.py:131
  11.6 36.8 %copy-start.23 = (f32[512]{0:T(512)S(1)}, f32[512]{0:T(512)}, u32[]{:S(2)}) copy-start(f32[512]{0:T(512)} %param.18) | copy-start | bytes 6148
  12.6 42.4 %copy-start.13 = (bf16[512,512]{1,0:T(8,128)(2,1)S(1)}, bf16[512,512]{1,0:T(8,128)(2,1)}, u32[]{:S(2)}) copy-start(bf16[512,512]{1,0:T(8,128)(2,1)} %param.21) | copy-start | bytes 1572868
  12.9 34.9 %copy-start.8 = (bf16[192,512]{1,0:T(8,128)(2,1)}, bf16[192,512]{1,0:T(8,128)(2,1)S(1)}, u32[]{:S(2)}) copy-start(bf16[192,512]{1,0:T(8,128)(2,1)S(1)} %get-tuple-element.15) | copy-start | bytes 589828
  47.8 0.6 copy-start.27
  47.8 0.6 copy-start.25
  48.5 6.9 %copy-start.11 = (bf16[512,512]{1,0:T(8,128)(2,1)S(1)}, bf16[512,512]{1,0:T(8,128)(2,1)}, u32[]{:S(2)}) copy-start(bf16[512,512]{1,0:T(8,128)(2,1)} %param.20) | copy-start | bytes 1572868
  57.1 0.9 copy-start.17
  57.1 146.3 %reduce-scatter.13.cloned.1.call-start = ((), (), s32[]{:S(2)}) async-start(), calls=%async_computation.14 | async-start | bytes 6684672 | tf_op jit(solution)/shard_map/reduce_scatter | solution.py:112
  64.3 0.8 copy-start.4
  72.0 220.3 %reduce-scatter.9.cloned.1.call-start = ((), (), s32[]{:S(2)}) async-start(), calls=%async_computation.11 | async-start | bytes 6684672 | tf_op jit(solution)/shard_map/reduce_scatter | solution.py:112
  78.8 0.7 copy-start.2
  80.8 0.9 copy-start.30
  80.9 223.9 %copy-start.32 = (pred[8]{0:T(512)(128)(4,1)}, pred[8]{0:T(512)(128)(4,1)S(1)}, u32[]{:S(2)}) copy-start(pred[8]{0:T(512)(128)(4,1)S(1)} %get-tuple-element.12) | copy-start | bytes 28
  81.6 211.7 %copy-start.19 = (f32[24,64]{1,0:T(8,128)}, f32[24,64]{1,0:T(8,128)S(1)}, u32[]{:S(2)}) copy-start(f32[24,64]{1,0:T(8,128)S(1)} %get-tuple-element.33) | copy-start | bytes 18436
  81.7 223.8 %copy-start.21 = (pred[96,384]{1,0:T(8,128)(4,1)}, pred[96,384]{1,0:T(8,128)(4,1)S(1)}, u32[]{:S(2)}) copy-start(pred[96,384]{1,0:T(8,128)(4,1)S(1)} %fusion.53) | copy-start | bytes 110596
  205.1 89.4 %all-to-all-start.2 = ((bf16[24,4,1024]{2,0,1:T(8,128)(2,1)}), bf16[24,4,1024]{2,0,1:T(8,128)(2,1)S(1)}, u32[]{:S(2)}, u32[]{:S(2)}) async-start(bf16[24,4,1024]{2,0,1:T(8,128)(2,1)} %bitcast.90), calls=%async_computation.6 | async-start | bytes 393216 | tf_op jit(solution)/shard_map/all_to_all | solution.py:118
  294.5 8.7 %all-to-all-start = ((bf16[24,4,1024]{2,0,1:T(8,128)(2,1)}), bf16[24,4,1024]{2,0,1:T(8,128)(2,1)S(1)}, u32[]{:S(2)}, u32[]{:S(2)}) async-start(bf16[24,4,1024]{2,0,1:T(8,128)(2,1)} %copy.62), calls=%async_computation.2 | async-start | bytes 393216 | tf_op jit(solution)/shard_map/all_to_all | solution.py:118
  297.9 78.7 %reduce-scatter.15.cloned.1.call-start = ((), (), s32[]{:S(2)}) async-start(), calls=%async_computation.16 | async-start | bytes 835584 | tf_op jit(solution)/shard_map/reduce_scatter | solution.py:217
  299.0 4.2 copy-start.6
  299.7 5.0 copy-start.15
  305.5 1.7 copy-start.34
  305.5 1.7 copy-start.36
  313.6 2.0 copy-start.29
  320.5 1.4 copy-start.31
  320.5 1.6 copy-start.16
  320.5 1.6 copy-start.22
  320.5 1.6 copy-start.33
  320.5 1.6 copy-start.35
  320.5 1.8 copy-start.37
  321.6 103.1 %all-gather.5.cloned.1.call-start = ((), (), s32[]{:S(2)}) async-start(), calls=%async_computation.15 | async-start | bytes 3342336 | tf_op jit(solution)/shard_map/all_gather | solution.py:124
  328.4 8.8 %copy-start.7 = (bf16[8,384,128]{2,1,0:T(8,128)(2,1)S(1)}, bf16[8,384,128]{2,1,0:T(8,128)(2,1)}, u32[]{:S(2)}) copy-start(bf16[8,384,128]{2,1,0:T(8,128)(2,1)} %copy-done.6) | copy-start | bytes 2359300
  337.2 134.5 %all-gather.3.cloned.1.call-start = ((), (), s32[]{:S(2)}) async-start(), calls=%async_computation.12 | async-start | bytes 3342336 | tf_op jit(solution)/shard_map/all_gather | solution.py:124
  337.7 39.6 %copy-start.20 = (f32[24,64]{1,0:T(8,128)S(1)}, f32[24,64]{1,0:T(8,128)}, u32[]{:S(2)}) copy-start(f32[24,64]{1,0:T(8,128)} %copy-done.19) | copy-start | bytes 18436
  346.3 142.8 %reduce-scatter.17.cloned.1.call-start = ((), (), s32[]{:S(2)}) async-start(), calls=%async_computation.17 | async-start | bytes 589824 | tf_op jit(solution)/shard_map/reduce_scatter | solution.py:255
  401.0 28.7 %copy-start.12 = (bf16[512,512]{1,0:T(8,128)(2,1)S(1)}, bf16[512,512]{1,0:T(8,128)(2,1)}, u32[]{:S(2)}) copy-start(bf16[512,512]{1,0:T(8,128)(2,1)} %param.20) | copy-start | bytes 1572868
  429.6 1.0 copy-start.14
  431.9 95.4 %reduce-scatter.11.cloned.1.call-start = ((), (), s32[]{:S(2)}) async-start(), calls=%async_computation.13 | async-start | bytes 589824 | tf_op jit(solution)/shard_map/reduce_scatter | solution.py:174
  471.6 5.8 %copy-start.10 = (bf16[384,4096]{1,0:T(8,128)(2,1)S(1)}, bf16[384,4096]{1,0:T(8,128)(2,1)}, u32[]{:S(2)}) copy-start(bf16[384,4096]{1,0:T(8,128)(2,1)} %all-gather.5.cloned.1.call-done) | copy-start | bytes 9437188
  477.5 5.8 %copy-start.3 = (bf16[384,4096]{1,0:T(8,128)(2,1)S(1)}, bf16[384,4096]{1,0:T(8,128)(2,1)}, u32[]{:S(2)}) copy-start(bf16[384,4096]{1,0:T(8,128)(2,1)} %all-gather.3.cloned.1.call-done) | copy-start | bytes 9437188
  477.5 5.8 %copy-start.5 = (bf16[384,512]{1,0:T(8,128)(2,1)S(1)}, bf16[384,512]{1,0:T(8,128)(2,1)}, u32[]{:S(2)}) copy-start(bf16[384,512]{1,0:T(8,128)(2,1)} %copy-done.4) | copy-start | bytes 1179652
  483.3 5.9 %copy-start.9 = (bf16[192,512]{1,0:T(8,128)(2,1)S(1)}, bf16[192,512]{1,0:T(8,128)(2,1)}, u32[]{:S(2)}) copy-start(bf16[192,512]{1,0:T(8,128)(2,1)} %copy-done.8) | copy-start | bytes 589828
  483.3 5.9 %copy-start.24 = (f32[512]{0:T(512)S(1)}, f32[512]{0:T(512)}, u32[]{:S(2)}) copy-start(f32[512]{0:T(512)} %param.18) | copy-start | bytes 6148
  483.3 5.9 %copy-start.26 = (f32[192]{0:T(256)S(1)}, f32[192]{0:T(256)}, u32[]{:S(2)}) copy-start(f32[192]{0:T(256)} %copy-done.25) | copy-start | bytes 2308
  483.3 43.9 %copy-start.28 = (f32[192]{0:T(256)S(1)}, f32[192]{0:T(256)}, u32[]{:S(2)}) copy-start(f32[192]{0:T(256)} %copy-done.27) | copy-start | bytes 2308
  483.3 44.0 %copy-start.18 = (bf16[192,512]{1,0:T(8,128)(2,1)S(1)}, bf16[192,512]{1,0:T(8,128)(2,1)}, u32[]{:S(2)}) copy-start(bf16[192,512]{1,0:T(8,128)(2,1)} %param.23) | copy-start | bytes 589828
  483.3 46.0 %copy-start.1 = (bf16[1024,512]{1,0:T(8,128)(2,1)S(1)}, bf16[1024,512]{1,0:T(8,128)(2,1)}, u32[]{:S(2)}) copy-start(bf16[1024,512]{1,0:T(8,128)(2,1)} %param.17) | copy-start | bytes 3145732
Sparse Core Ops, SparseCore 0:
  57.2 56.8 reduce-scatter.6
  119.1 84.2 reduce-scatter.12
  207.9 84.3 reduce-scatter.8
  321.7 54.7 reduce-scatter.14
  379.2 45.3 all-gather.4
  427.4 44.2 all-gather.2
  473.9 11.9 reduce-scatter.16
  488.2 13.1 reduce-scatter.10
where the time goes:
time: 537 us; the launch traced here: 536 us
  waiting for transfers between devices  277 us (52%)
  blocking collectives  144 us (27%)
  matrix products  57.4 us (11%)
  local copies, waits for them, and re-layouts  18.4 us (3%)
  other arithmetic  16.6 us (3%)
  between operations  14.9 us (3%)
  starting transfers between devices  7.73 us (1%)
    reduce_scatter x2, waiting for transfers between devices, to_heads(): lax.psum_scatter(term(jnp.int32(0), block_len * lax.axis_size(('row', 'se...  150 us
    all_gather x2, waiting for transfers between devices, to_rows(): return lax.all_gather(own_share, ('row', 'seq'), axis=0, tiled=True)  61.7 us
    psum x1, blocking collectives, per_device(): squares = lax.psum(jnp.sum(residual * residual, axis=1), ('row', 'seq'))  34.9 us
    reduce_scatter x1, waiting for transfers between devices, per_device(): lax.psum_scatter(jnp.concatenate([jnp.dot(picked, w_key, preferred_elemen...  32.3 us
    psum x1, blocking collectives, per_device(): lax.psum(jnp.sum(scaled_grad * residual, axis=1), ('row', 'seq'))  31.5 us
    reduce_scatter x1, waiting for transfers between devices, per_device(): lax.psum_scatter(jnp.concatenate([grad_key_part, grad_value_part], axis=1...  30.2 us
    all_gather x1, blocking collectives, per_device(): lax.all_gather(kv_grad_block, ('row', 'seq'), axis=0, tiled=True)  22 us
    all_gather x1, blocking collectives, per_device(): kv_all = lax.all_gather(kv_block, ('row', 'seq'), axis=0, tiled=True)  21.5 us
  transfers between devices with their start and end apart: 10, of which 7 were waited for; matrix products, arithmetic and copies ran while one was open for 11% of the time, Pallas kernels for 0%

commit v1 on v0

--- a/solution.py
+++ b/solution.py
@@ -65,7 +65,7 @@
     return values.astype(jnp.bfloat16)
 
 
-def per_device(
+def general_device(
     motion_ids,
     audio_ids,
     segment_ids,
@@ -274,6 +274,172 @@
     return (layer_out, grad_input, grad_gain, grad_wq, grad_wk, grad_wv, grad_wo)
 
 
+def fast_device(
+    motion_ids,
+    audio_ids,
+    segment_ids,
+    motion_table,
+    audio_table,
+    norm_gain,
+    w_query,
+    w_key,
+    w_value,
+    w_out,
+    out_grad,
+):
+    f32, bf16 = jnp.float32, jnp.bfloat16
+    seq_len = segment_ids.shape[0]
+    row_devices = lax.axis_size("row")
+    seq_devices = lax.axis_size("seq")
+    groups = row_devices * seq_devices
+    row_index = lax.axis_index("row")
+    seq_index = lax.axis_index("seq")
+    col_index = lax.axis_index("col")
+    own_len = out_grad.shape[0]
+    model_width = out_grad.shape[1]
+    query_width = w_query.shape[1]
+    kv_width = w_key.shape[1]
+    head_count = query_width // HD // groups
+    kv_len = seq_len // seq_devices
+    score_scale = HD ** (-0.5)
+
+    embedded = (
+        jnp.take(motion_table, motion_ids, axis=0).astype(f32)
+        + jnp.take(audio_table, audio_ids, axis=0).astype(f32)
+    ).astype(bf16)
+    both = lax.all_gather(
+        jnp.concatenate([embedded, out_grad], axis=1), "col", axis=0, tiled=True
+    )
+    embedded_all = both[:, :model_width]
+    grad_all = both[:, model_width:]
+    residual_all = embedded_all.astype(f32)
+    squares = lax.psum(jnp.sum(residual_all * residual_all, axis=1), ("row", "seq"))
+    inverse = lax.rsqrt(squares / D + epsilon)
+    scaled = (residual_all * norm_gain[None, :]).astype(bf16)
+
+    def product(left, right):
+        return jnp.dot(left, right, preferred_element_type=f32).astype(bf16)
+
+    kv_part = jnp.concatenate(
+        [
+            product(scaled, w_key).reshape(seq_len, row_devices, HD),
+            product(scaled, w_value).reshape(seq_len, row_devices, HD),
+        ],
+        axis=2,
+    ).reshape(seq_len, 2 * kv_width)
+    kv_sum = lax.psum(
+        lax.psum_scatter(kv_part, "row", scatter_dimension=1, tiled=True), "seq"
+    ).astype(f32)
+    query_sum = lax.psum_scatter(
+        product(scaled, w_query), ("row", "seq"), scatter_dimension=1, tiled=True
+    ).astype(f32)
+    out_part = jnp.einsum("ld,nd->ln", grad_all, w_out, preferred_element_type=f32).astype(bf16)
+    out_heads = lax.psum_scatter(
+        out_part, ("row", "seq"), scatter_dimension=1, tiled=True
+    ).reshape(seq_len, head_count, HD)
+
+    positions = jnp.arange(seq_len, dtype=jnp.int32)
+    cosines, sines = rotary_tables(positions, HD)
+    query_heads = rotate_pairs(
+        (query_sum * inverse[:, None]).reshape(seq_len, head_count, HD), cosines, sines
+    ).astype(bf16)
+    kv_scaled = kv_sum * inverse[:, None]
+    keys = rotate_pairs(kv_scaled[:, None, :HD], cosines, sines)[:, 0].astype(bf16)
+    values = kv_scaled[:, HD:].astype(bf16)
+
+    allowed = (positions[None, :] <= positions[:, None]) & (
+        segment_ids[None, :] == segment_ids[:, None]
+    )
+    raw_scores = jnp.einsum("qhd,kd->hqk", query_heads, keys, preferred_element_type=f32)
+    tanh_scores = jnp.tanh(raw_scores * (score_scale / softcap))
+    weights = jnp.where(allowed[None], jnp.exp(softcap * tanh_scores), 0.0)
+    totals = jnp.sum(weights, axis=2)
+    attended = jnp.einsum(
+        "hqk,kd->qhd", weights.astype(bf16), values, preferred_element_type=f32
+    )
+    attn_out = (attended / totals.T[:, :, None]).astype(bf16).reshape(seq_len, head_count * HD)
+    out_all = lax.all_gather(attn_out, ("row", "seq"), axis=1, tiled=True)
+
+    probs = weights / totals[:, :, None]
+    prob_grads = jnp.einsum("qhd,kd->hqk", out_heads, values, preferred_element_type=f32)
+    row_dots = jnp.sum(probs * prob_grads, axis=2, keepdims=True)
+    grad_scores = (
+        probs * (prob_grads - row_dots) * (1.0 - tanh_scores**2) * score_scale
+    ).astype(bf16)
+    grad_query = jnp.einsum("hqk,kd->qhd", grad_scores, keys, preferred_element_type=f32)
+    grad_key = jnp.einsum("hqk,qhd->kd", grad_scores, query_heads, preferred_element_type=f32)
+    grad_value = jnp.einsum(
+        "hqk,qhd->kd", probs.astype(bf16), out_heads, preferred_element_type=f32
+    )
+    dot_query = jnp.sum(grad_query * query_heads.astype(f32), axis=(1, 2))
+    grad_query_own = (
+        rotate_back(grad_query, cosines, sines).astype(bf16).reshape(seq_len, head_count * HD)
+    )
+    kv_first = seq_index * kv_len
+    kv_grad = lax.psum_scatter(
+        jnp.concatenate([grad_key, grad_value], axis=1).astype(bf16),
+        "seq",
+        scatter_dimension=0,
+        tiled=True,
+    ).astype(f32)
+
+    def own_rows(array):
+        return lax.dynamic_slice_in_dim(array, kv_first, kv_len, axis=0)
+
+    kv_own = own_rows(jnp.concatenate([keys, values], axis=1)).astype(f32)
+    dot_kv = jnp.sum(kv_grad * kv_own, axis=1)
+    dot_part = lax.dynamic_update_slice_in_dim(
+        dot_query, own_rows(dot_query) + dot_kv, kv_first, axis=0
+    )
+    grad_key_own = rotate_back(kv_grad[:, None, :HD], own_rows(cosines), own_rows(sines))[:, 0]
+    kv_grad_own = jnp.concatenate([grad_key_own, kv_grad[:, HD:]], axis=1).astype(bf16)
+    kv_grad_all = lax.all_gather(
+        lax.all_gather(kv_grad_own, "seq", axis=0, tiled=True), "row", axis=1, tiled=False
+    )
+    grad_query_all = lax.all_gather(grad_query_own, ("row", "seq"), axis=1, tiled=True)
+    grad_key_all = kv_grad_all[:, :, :HD].reshape(seq_len, kv_width)
+    grad_value_all = kv_grad_all[:, :, HD:].reshape(seq_len, kv_width)
+
+    dot_sum = lax.psum(dot_part, ("row", "seq", "col"))
+    normed = (residual_all * inverse[:, None] * norm_gain[None, :]).astype(bf16)
+    branch_part = product(out_all, w_out)
+    grad_wo = jnp.einsum("ln,ld->nd", out_all, grad_all, preferred_element_type=f32)
+    grad_wq = jnp.einsum("ld,ln->dn", normed, grad_query_all, preferred_element_type=f32)
+    grad_wk = jnp.einsum("ld,ln->dn", normed, grad_key_all, preferred_element_type=f32)
+    grad_wv = jnp.einsum("ld,ln->dn", normed, grad_value_all, preferred_element_type=f32)
+    normed_part = (
+        jnp.einsum("ln,dn->ld", grad_query_all, w_query, preferred_element_type=f32)
+        + jnp.einsum("ln,dn->ld", grad_key_all, w_key, preferred_element_type=f32)
+        + jnp.einsum("ln,dn->ld", grad_value_all, w_value, preferred_element_type=f32)
+    )
+    gain_part = jnp.sum(normed_part * residual_all * inverse[:, None], axis=0)
+    branch_sum, grad_normed = (
+        lax.psum_scatter(
+            jnp.concatenate([branch_part, normed_part.astype(bf16)], axis=1),
+            "col",
+            scatter_dimension=0,
+            tiled=True,
+        )
+        .astype(f32)
+        .reshape(own_len, 2, model_width)
+        .swapaxes(0, 1)
+    )
+    grad_gain = lax.psum(gain_part, "col")
+
+    def own_part(array):
+        return lax.dynamic_slice_in_dim(array, col_index * own_len, own_len, axis=0)
+
+    residual = embedded.astype(f32)
+    inverse_own = own_part(inverse)[:, None]
+    layer_out = (residual + branch_sum).astype(bf16)
+    grad_input = (
+        out_grad.astype(f32)
+        + inverse_own * (grad_normed * norm_gain[None, :])
+        - residual * (inverse_own**2 * own_part(dot_sum)[:, None] / D)
+    ).astype(bf16)
+    return (layer_out, grad_input, grad_gain, grad_wq, grad_wk, grad_wv, grad_wo)
+
+
 def solution(mesh):
     placed = (
         P("col"),
@@ -288,8 +454,15 @@
         P("col", ("row", "seq")),
         P("col", ("row", "seq")),
     )
+    groups = mesh.shape["row"] * mesh.shape["seq"]
+    heads_col = H // mesh.shape["col"]
+    whole_heads = (
+        heads_col % groups == 0
+        and KV // mesh.shape["col"] == mesh.shape["row"]
+        and mesh.shape["seq"] == 4
+    )
     return jax.shard_map(
-        per_device,
+        fast_device if whole_heads else general_device,
         mesh=mesh,
         in_specs=placed,
         out_specs=(

time: 537 us -> 352 us (0.66)
  waiting for transfers between devices: 277 us -> 129 us
  blocking collectives: 144 us -> 125 us
  starting transfers between devices: 7.73 us -> 0.52 us
    reduce_scatter x6 -> x4, waiting for transfers between devices: 212 us -> 118 us  [the longest x1 66.2 us: fast_device(): lax.psum_scatter(out_part, ('row', 'seq'), scatter_dimension=1, tiled=True)]
    all_gather x2, waiting for transfers between devices: 61.7 us -> 0.71 us  [the longest x1 0.68 us: fast_device(): out_all = lax.all_gather(attn_out, ('row', 'seq'), axis=1, tiled=True)]
    all_to_all x2 -> x0, blocking collectives: 15.4 us -> none  [to_rows(): lax.all_to_all(heads_part, 'seq', split_axis=0, concat_axis=1, tiled=True)]
    unnamed x8 -> x9, waiting for transfers between devices: 0.13 us -> 10.1 us
    all_gather x4 -> x3, blocking collectives: 56.3 us -> 47.4 us  [the longest x1 29.1 us: fast_device(): lax.all_gather(lax.all_gather(kv_grad_own, 'seq', axis=0, tiled=True), 'r...]
    all_to_all x2 -> x0, starting transfers between devices: 6.73 us -> none  [to_heads(): lax.all_to_all(finish(own_share, block_pos), 'seq', split_axis=1, concat_...]
    psum x3, blocking collectives: 71.8 us -> 77.6 us  [the longest x1 40.4 us: fast_device(): dot_sum = lax.psum(dot_part, ('row', 'seq', 'col'))]
  transfers between devices with their start and end apart: 10 -> 8, of which waited for: 7 -> 5; matrix products, arithmetic and copies ran while one was open for 11% -> 15% of each run, Pallas kernels for 0% -> 0%
where the time goes in v1:
time: 352 us; the launch traced here: 351 us
  waiting for transfers between devices  129 us (37%)
  blocking collectives  125 us (36%)
  matrix products  53.2 us (15%)
  between operations  16 us (5%)
  local copies, waits for them, and re-layouts  15.9 us (5%)
  other arithmetic  12 us (3%)
    reduce_scatter x1, waiting for transfers between devices, fast_device(): lax.psum_scatter(out_part, ('row', 'seq'), scatter_dimension=1, tiled=True)  66.2 us
    psum x1, blocking collectives, fast_device(): dot_sum = lax.psum(dot_part, ('row', 'seq', 'col'))  40.4 us
    psum x1, blocking collectives, fast_device(): lax.psum(jnp.sum(residual_all * residual_all, axis=1), ('row', 'seq'))  31.5 us
    all_gather x1, blocking collectives, fast_device(): lax.all_gather(lax.all_gather(kv_grad_own, 'seq', axis=0, tiled=True), 'r...  29.1 us
    reduce_scatter x1, waiting for transfers between devices, fast_device(): lax.psum_scatter(product(scaled, w_query), ('row', 'seq'), scatter_dimens...  26.6 us
    reduce_scatter x1, waiting for transfers between devices, fast_device(): lax.psum_scatter(kv_part, 'row', scatter_dimension=1, tiled=True)  24.9 us
    all_gather x1, blocking collectives, fast_device(): lax.all_gather(jnp.concatenate([embedded, out_grad], axis=1), 'col', axis...  12.8 us
    dot_general x4, matrix products, product(): return jnp.dot(left, right, preferred_element_type=f32).astype(bf16)  11.9 us
  transfers between devices with their start and end apart: 8, of which 5 were waited for; matrix products, arithmetic and copies ran while one was open for 15% of the time, Pallas kernels for 0%

profile of v1, /device:TPU:0, one launch (start us, length us, event | category | flops | bytes accessed | tf_op | source)
XLA Modules:
  0.0 351.1 jit_solution(17718531531862818762)
XLA Ops:
  8.1 0.8 compare_and_fusion
  8.8 0.7 compare_select_fusion
  9.6 2.2 gather_fusion
  11.7 1.0 gather_fusion.1
  12.9 0.7 copy-done.2
  13.6 12.8 %all_gather.18 = bf16[384,1024]{1,0:T(8,128)(2,1)S(1)} all-gather(bf16[192,1024]{1,0:T(8,128)(2,1)S(1)} %pad_maximum_fusion.2), channel_id=1, replica_groups=mesh['row'=4,'col'=2,'seq'=4] {'col'}, dimensions={0}, use_global_device_ids=true | all-gather | bytes 1179648 | tf_op jit(solution)/shard_map/all_gather | solution.py:310
  28.0 1.0 pad_maximum_fusion
  29.1 24.9 %reduce-scatter.8.cloned.1.call-done = bf16[384,256]{0,1:T(8,128)(2,1)} async-done(((bf16[384,1024]{0,1:T(8,128)(2,1)}), bf16[384,256]{0,1:T(8,128)(2,1)}) %reduce-scatter.8.cloned.1.call-update) | async-done | bytes 196624 | tf_op jit(solution)/shard_map/reduce_scatter | solution.py:331
  54.0 6.2 %convolution_convert_fusion.1 = bf16[384,4096]{0,1:T(8,128)(2,1)} fusion(bf16[512,4096]{1,0:T(8,128)(2,1)} %param.17, f32[512]{0:T(512)S(1)} %copy-done.17, bf16[384,1024]{1,0:T(8,128)(2,1)S(1)} %all_gather.18), kind=kOutput, calls=%fused_computation.4 | convolution fusion | flops 1612775424 | bytes 7735296 | tf_op jit(solution)/shard_map/dot_general | solution.py:321
  60.4 5.7 %convolution_convert_fusion = bf16[384,4096]{1,0:T(8,128)(2,1)} fusion(bf16[4096,512]{1,0:T(8,128)(2,1)} %param.20, bf16[384,1024]{1,0:T(8,128)(2,1)S(1)} %all_gather.18), kind=kOutput, calls=%fused_computation.3 | convolution fusion | flops 1612185600 | bytes 7733248 | tf_op jit(solution)/shard_map/ld,nd->ln/dot_general | solution.py:336
  67.0 31.5 %psum.29 = f32[384]{0:T(512)S(1)} all-reduce(f32[384]{0:T(512)S(1)} %fusion.17), channel_id=1, replica_groups=mesh['row'=4,'col'=2,'seq'=4] {'row','seq'}, use_global_device_ids=true, to_apply=%region_3.4 | all-reduce | flops 384 | bytes 3072 | tf_op jit(solution)/shard_map/psum | solution.py:316
  98.6 0.8 fusion.33
  99.4 26.6 %reduce-scatter.10.cloned.1.call-done = bf16[384,256]{0,1:T(8,128)(2,1)} async-done(((bf16[384,4096]{0,1:T(8,128)(2,1)}), bf16[384,256]{0,1:T(8,128)(2,1)}) %reduce-scatter.10.cloned.1.call-update) | async-done | bytes 196624 | tf_op jit(solution)/shard_map/reduce_scatter | solution.py:333
  125.9 1.1 convert_multiply_fusion.5
  127.0 0.7 fusion.98
  127.9 1.1 copy.103
  129.4 66.2 %reduce-scatter.12.cloned.1.call-done = bf16[384,256]{1,0:T(8,128)(2,1)} async-done(((bf16[384,4096]{1,0:T(8,128)(2,1)}), bf16[384,256]{1,0:T(8,128)(2,1)}) %reduce-scatter.12.cloned.1.call-update) | async-done | bytes 196624 | tf_op jit(solution)/shard_map/reduce_scatter | solution.py:337
  195.7 1.7 copy.105
  197.4 2.3 convolution_bitcast_fusion
  199.8 0.8 copy-done.15
  200.6 0.7 fusion.23
  201.3 1.0 copy-done.21
  203.3 3.5 %fusion.9 = bf16[384,128]{0,1:T(8,128)(2,1)S(1)} fusion(f32[2,384,384]{1,2,0:T(8,128)} %convolution_bitcast_fusion, f32[384,384,2]{1,0,2:T(8,128)} %copy-done.21, bf16[384,2,64]{2,0,1:T(8,128)(2,1)S(1)} %copy-done.14, bf16[384,2,64]{2,0,1:T(8,128)(2,1)S(1)} %copy-done.12, f32[2,384]{1,0:T(2,128)S(1)} %get-tuple-element.29, pred[384,384]{0,1:T(8,128)(4,1)} %fusion.33), kind=kOutput, calls=%fused_computation.29 | convolution fusion | flops 80069760 | bytes 2804736 | tf_op jit(solution)/shard_map/hqk,qhd->kd/dot_general | solution.py:370
  206.9 0.8 copy.101
  208.0 3.6 %multiply_reduce_fusion.1 = (f32[384]{0:T(512)S(1)}, f32[384,2,128]{2,0,1:T(8,128)S(1)}) fusion(bf16[384,2,64]{2,0,1:T(8,128)(2,1)S(1)} %copy-done.14, bf16[384,2,64]{2,0,1:T(8,128)(2,1)S(1)} %copy-done.12, f32[2,384,384]{1,2,0:T(8,128)} %convolution_bitcast_fusion, f32[384,384,2]{1,0,2:T(8,128)} %copy-done.21, f32[2,384]{1,0:T(2,128)S(1)} %get-tuple-element.29, ...), kind=kOutput, calls=%fused_computation.72 | convolution fusion | flops 80413440 | bytes 3199488 | tf_op jit(solution)/shard_map/hqk,kd->qhd/dot_general | solution.py:369
  211.9 0.8 copy.81
  212.8 2.4 fusion.8
  215.2 0.7 slice.123
  215.9 0.7 fusion.77
  216.5 10.0 %reduce-scatter.16.cloned.1.call-done = bf16[96,256]{1,0:T(8,128)(2,1)} async-done(((bf16[384,256]{1,0:T(8,128)(2,1)}), bf16[96,256]{1,0:T(8,128)(2,1)}) %reduce-scatter.16.cloned.1.call-update) | async-done | bytes 49168
  226.5 0.9 copy.102
  227.5 1.0 fusion.74
  228.6 5.6 %all_gather.21 = bf16[384,256]{1,0:T(8,128)(2,1)S(1)} all-gather(bf16[96,256]{1,0:T(8,128)(2,1)S(1)} %copy.86), channel_id=1, replica_groups=mesh['row'=4,'col'=2,'seq'=4] {'seq'}, dimensions={0}, use_global_device_ids=true | all-gather | bytes 245760 | tf_op jit(solution)/shard_map/all_gather | solution.py:397
  234.2 29.1 %all-gather = bf16[384,1024]{1,0:T(8,128)(2,1)S(1)} all-gather(bf16[384,256]{1,0:T(8,128)(2,1)S(1)} %all_gather.21), channel_id=2, replica_groups=mesh['row'=4,'col'=2,'seq'=4] {'row'}, dimensions={1}, use_global_device_ids=true | all-gather | bytes 983040 | tf_op jit(solution)/shard_map/all_gather | solution.py:396
  263.9 1.0 multiply_reduce_fusion.2
  265.1 40.4 %psum.30 = f32[384]{0:T(512)S(1)} all-reduce(f32[384]{0:T(512)S(1)} %add_dynamic-update-slice_fusion), channel_id=1, replica_groups=mesh['row'=4,'col'=2,'seq'=4] {'row','seq','col'}, use_global_device_ids=true, to_apply=%region_12.13 | all-reduce | flops 384 | bytes 3072 | tf_op jit(solution)/shard_map/psum | solution.py:403
  305.9 5.1 %fusion.103 = f32[384,512]{1,0:T(8,128)S(1)} fusion(bf16[384,4096]{0,1:T(8,128)(2,1)} %all-gather.6.cloned.1.call-done, bf16[512,4096]{1,0:T(8,128)(2,1)} %param.17), kind=kOutput, calls=%fused_computation.154 | convolution fusion | flops 1610612736 | bytes 8126464 | tf_op jit(solution)/shard_map/ln,dn->ld/dot_general | solution.py:411
  311.4 0.7 copy-done.20
  312.5 0.7 all-gather.4.cloned.1.call-done
  313.2 5.0 %convolution_convert_fusion.4 = bf16[384,512]{1,0:T(8,128)(2,1)S(1)} fusion(bf16[384,4096]{0,1:T(8,128)(2,1)} %all-gather.4.cloned.1.call-done, bf16[4096,512]{1,0:T(8,128)(2,1)} %param.20), kind=kOutput, calls=%fused_computation.21 | convolution fusion | flops 1610809344 | bytes 7733248 | tf_op jit(solution)/shard_map/dot_general | solution.py:321
  318.1 1.0 pad_maximum_fusion.1
  319.2 1.5 fusion.38
  320.7 1.5 fusion.41
  322.2 5.7 %psum.31 = f32[512]{0:T(512)} all-reduce(f32[512]{0:T(512)S(1)} %get-tuple-element.13), channel_id=1, replica_groups=mesh['row'=4,'col'=2,'seq'=4] {'col'}, use_global_device_ids=true, to_apply=%region_14.15 | all-reduce | flops 512 | bytes 4096 | tf_op jit(solution)/shard_map/psum | solution.py:427
  327.9 7.8 %fusion.51 = f32[4096,512]{1,0:T(8,128)} fusion(bf16[384,4096]{0,1:T(8,128)(2,1)} %all-gather.4.cloned.1.call-done, bf16[384,1024]{1,0:T(8,128)(2,1)S(1)} %all_gather.18), kind=kOutput, calls=%fused_computation.84 | convolution fusion | flops 1610612736 | bytes 11927552 | tf_op jit(solution)/shard_map/ln,ld->nd/dot_general | solution.py:406
  335.7 5.9 %fusion.90 = f32[512,4096]{1,0:T(8,128)} fusion(bf16[384,4096]{0,1:T(8,128)(2,1)S(1)} %copy-done.1, f32[384]{0:T(512)S(1)} %add_rsqrt_fusion, f32[512]{0:T(512)S(1)} %copy-done.17, bf16[384,1024]{1,0:T(8,128)(2,1)S(1)} %all_gather.18), kind=kOutput, calls=%fused_computation.149 | convolution fusion | flops 1611399168 | bytes 11931648 | tf_op jit(solution)/shard_map/ld,ln->dn/dot_general | solution.py:407
  341.6 1.1 transpose.68
  342.9 0.9 fusion.37
  (95 shorter events, 7.7 us)
Async XLA Ops:
  8.0 3.7 %copy-start = (bf16[1024,512]{1,0:T(8,128)(2,1)S(1)}, bf16[1024,512]{1,0:T(8,128)(2,1)}, u32[]{:S(2)}) copy-start(bf16[1024,512]{1,0:T(8,128)(2,1)} %param.15) | copy-start | bytes 3145732
  8.0 45.9 %reduce-scatter.8.cloned.1.call-start = ((), (), s32[]{:S(2)}) async-start(), calls=%async_computation.5 | async-start | bytes 983040 | tf_op jit(solution)/shard_map/reduce_scatter | solution.py:331
  11.7 1.9 copy-start.5
  12.7 13.7 %copy-start.17 = (f32[512]{0:T(512)S(1)}, f32[512]{0:T(512)}, u32[]{:S(2)}) copy-start(f32[512]{0:T(512)} %param.16) | copy-start | bytes 6148
  12.8 13.6 %copy-start.19 = (bf16[512,512]{1,0:T(8,128)(2,1)S(1)}, bf16[512,512]{1,0:T(8,128)(2,1)}, u32[]{:S(2)}) copy-start(bf16[512,512]{1,0:T(8,128)(2,1)} %param.19) | copy-start | bytes 1572868
  12.9 0.7 copy-start.2
  26.4 1.0 copy-start.9
  29.0 70.3 %all-reduce.2.cloned.1.call-start = ((), (), s32[]{:S(2)}) async-start(), calls=%async_computation.6 | async-start | bytes 393216 | tf_op jit(solution)/shard_map/psum | solution.py:330
  54.0 71.9 %reduce-scatter.10.cloned.1.call-start = ((), (), s32[]{:S(2)}) async-start(), calls=%async_computation.7 | async-start | bytes 3342336 | tf_op jit(solution)/shard_map/reduce_scatter | solution.py:333
  60.3 135.4 %reduce-scatter.12.cloned.1.call-start = ((), (), s32[]{:S(2)}) async-start(), calls=%async_computation.9 | async-start | bytes 3342336 | tf_op jit(solution)/shard_map/reduce_scatter | solution.py:337
  66.1 32.5 %copy-start.18 = (s32[384]{0:T(512)S(1)}, s32[384]{0:T(512)}, u32[]{:S(2)}) copy-start(s32[384]{0:T(512)} %param.13) | copy-start | bytes 4612
  66.1 160.4 %reduce-scatter.16.cloned.1.call-start = ((), (), s32[]{:S(2)}) async-start(), calls=%async_computation.12 | async-start | bytes 245760
  66.6 32.8 %copy-start.7 = (f32[384,64]{0,1:T(8,128)}, f32[384,64]{0,1:T(8,128)S(1)}, u32[]{:S(2)}) copy-start(f32[384,64]{0,1:T(8,128)S(1)} %get-tuple-element.25) | copy-start | bytes 294916
  66.6 32.8 %copy-start.8 = (f32[384,64]{0,1:T(8,128)}, f32[384,64]{0,1:T(8,128)S(1)}, u32[]{:S(2)}) copy-start(f32[384,64]{0,1:T(8,128)S(1)} %get-tuple-element.26) | copy-start | bytes 294916
  199.7 0.9 copy-start.15
  199.8 1.5 copy-start.11
  199.8 1.5 copy-start.13
  200.6 1.7 copy-start.4
  201.3 1.0 copy-start.21
  202.3 0.9 copy-start.12
  202.3 1.0 copy-start.14
  207.7 98.1 %all-gather.6.cloned.1.call-start = ((), (), s32[]{:S(2)}) async-start(), calls=%async_computation.10 | async-start | bytes 3342336 | tf_op jit(solution)/shard_map/all_gather | solution.py:399
  211.5 1.3 copy-start.16
  212.7 100.4 %all-gather.4.cloned.1.call-start = ((), (), s32[]{:S(2)}) async-start(), calls=%async_computation.8 | async-start | bytes 3342336 | tf_op jit(solution)/shard_map/all_gather | solution.py:361
  215.2 126.5 %reduce-scatter.14.cloned.1.call-start = ((), (), s32[]{:S(2)}) async-start(), calls=%async_computation.11 | async-start | bytes 1179648 | tf_op jit(solution)/shard_map/reduce_scatter | solution.py:417
  305.8 5.1 %copy-start.10 = (bf16[512,512]{1,0:T(8,128)(2,1)S(1)}, bf16[512,512]{1,0:T(8,128)(2,1)}, u32[]{:S(2)}) copy-start(bf16[512,512]{1,0:T(8,128)(2,1)} %param.18) | copy-start | bytes 1572868
  310.9 1.1 copy-start.20
  327.9 7.8 %copy-start.1 = (bf16[384,4096]{0,1:T(8,128)(2,1)S(1)}, bf16[384,4096]{0,1:T(8,128)(2,1)}, u32[]{:S(2)}) copy-start(bf16[384,4096]{0,1:T(8,128)(2,1)} %all-gather.6.cloned.1.call-done) | copy-start | bytes 9437188
  341.6 1.2 copy-start.3
  341.6 1.2 copy-start.6
Sparse Core Ops, SparseCore 0:
  29.1 24.7 reduce-scatter.7
  56.3 30.9 all-reduce.1
  207.9 18.6 reduce-scatter.15
  319.3 17.2 reduce-scatter.13
Sparse Core Ops, SparseCore 1:
  60.4 65.5 reduce-scatter.9
  130.6 65.0 reduce-scatter.11
  212.8 53.7 all-gather.5
  269.8 43.4 all-gather.3

commit v2 on v1

--- a/solution.py
+++ b/solution.py
@@ -1,6 +1,8 @@
 import jax
 import jax.numpy as jnp
 from jax import lax
+from jax.experimental import pallas as pl
+from jax.experimental.pallas import tpu as pltpu
 from jax.sharding import PartitionSpec as P
 
 D = 8192
@@ -274,6 +276,431 @@
     return (layer_out, grad_input, grad_gain, grad_wq, grad_wk, grad_wv, grad_wo)
 
 
+VMEM_BYTES = 56 * 1024 * 1024
+
+
+def remote(source, target, send_sem, recv_sem, place):
+    copy = pltpu.make_async_remote_copy(
+        src_ref=source,
+        dst_ref=target,
+        send_sem=send_sem,
+        recv_sem=recv_sem,
+        device_id=place,
+        device_id_type=pl.DeviceIdType.MESH,
+    )
+    copy.start()
+    return copy
+
+
+def greet(places):
+    barrier = pltpu.get_barrier_semaphore()
+    for place in places:
+        pl.semaphore_signal(
+            barrier, inc=1, device_id=place, device_id_type=pl.DeviceIdType.MESH
+        )
+    pl.semaphore_wait(barrier, len(places))
+
+
+def neighbours():
+    row = lax.axis_index("row")
+    seq = lax.axis_index("seq")
+    rows = lax.axis_size("row")
+    across, core = seq // 2, seq % 2
+    plane = [(across, 1 - core), (1 - across, core), (1 - across, 1 - core)]
+    plane_ids = [{"row": row, "seq": 2 * a + c} for a, c in plane]
+    plane_slots = [2 * c + a for a, c in plane]
+    others = [(row + step) % rows for step in range(1, rows)]
+    row_ids = [{"row": other, "seq": seq} for other in others]
+    return row, across, core, plane_ids, plane_slots, others, row_ids
+
+
+def reduce_kernel(
+    q_part, o_part, kv_part, sq_part,
+    q_out, o_out, kv_out, sq_out,
+    q_rc, o_rc, kv_rc, q_a1, o_a1, kv_a1, q_rx, o_rx, kv_rx, q_a2, o_a2, kv_a2,
+    q_rz, o_rz, kv_rz, kv_own, kv_all, sq_send, sq_recv,
+    core_send, core_recv, x_send, x_recv, z_send, z_recv, kv_send, kv_recv, sq_ss, sq_rs,
+):
+    f32, bf16 = jnp.float32, jnp.bfloat16
+    row, across, core, plane_ids, plane_slots, others, row_ids = neighbours()
+    rows = len(others) + 1
+    core_id, x_id = plane_ids[0], plane_ids[1]
+    greet(plane_ids + row_ids)
+    seq_len = q_out.shape[0]
+    width = q_out.shape[1]
+    block = seq_len // 4
+    wide = 2 * width
+    half_len = seq_len // 2
+    pieces = [(None, 0)] + [(0, b) for b in range(4)] + [(1, b) for b in range(4)]
+    parts, rcs, a1s = (q_part, o_part), (q_rc, o_rc), (q_a1, o_a1)
+    rxs, a2s, rzs, outs = (q_rx, o_rx), (q_a2, o_a2), (q_rz, o_rz), (q_out, o_out)
+    core_copies, x_copies, z_copies = [], [], []
+
+    sq_copy = remote(sq_part, sq_recv.at[0], sq_ss.at[0], sq_rs.at[0], core_id)
+    for index, (which, b) in enumerate(pieces):
+        copies = []
+        if which is None:
+            source = kv_part.at[pl.ds(pl.multiple_of((1 - core) * half_len, half_len), half_len)]
+            copies.append(
+                remote(source, kv_rc, core_send.at[index, 0], core_recv.at[index, 0], core_id)
+            )
+        else:
+            lines = pl.ds(b * block, block)
+            for r in range(rows):
+                first = pl.multiple_of(r * 2 * wide + (1 - core) * wide, wide)
+                copies.append(
+                    remote(
+                        parts[which].at[lines, pl.ds(first, wide)],
+                        rcs[which].at[lines, pl.ds(r * wide, wide)],
+                        core_send.at[index, r],
+                        core_recv.at[index, r],
+                        core_id,
+                    )
+                )
+        core_copies.append(copies)
+
+    def core_stage(index):
+        which, b = pieces[index]
+        for copy in core_copies[index]:
+            copy.wait_recv()
+        if which is None:
+            own = kv_part[pl.ds(pl.multiple_of(core * half_len, half_len), half_len), :]
+            kv_a1[...] = (own.astype(f32) + kv_rc[...].astype(f32)).astype(bf16)
+            source = kv_a1.at[pl.ds(pl.multiple_of((1 - across) * block, block), block)]
+            target = kv_rx
+        else:
+            lines = pl.ds(b * block, block)
+            for r in range(rows):
+                for side in range(2):
+                    first = pl.multiple_of(r * 2 * wide + core * wide + side * width, width)
+                    total = parts[which][lines, pl.ds(first, width)].astype(f32) + rcs[which][
+                        lines, pl.ds(r * wide + side * width, width)
+                    ].astype(f32)
+                    a1s[which][side, lines, pl.ds(r * width, width)] = total.astype(bf16)
+            source = a1s[which].at[1 - across, lines]
+            target = rxs[which].at[lines]
+        x_copies.append(remote(source, target, x_send.at[index], x_recv.at[index], x_id))
+
+    def x_stage(index):
+        which, b = pieces[index]
+        x_copies[index].wait_recv()
+        lines = pl.ds(b * block, block)
+        if which is None:
+            held = kv_a1[pl.ds(pl.multiple_of(across * block, block), block), :]
+            got, kept, landing, span = kv_rx[...], kv_a2, kv_rz, pl.ds(0, block)
+        else:
+            held = a1s[which][across, lines, :]
+            got, kept, landing, span = rxs[which][lines, :], a2s[which], rzs[which], lines
+        total = (held.astype(f32) + got.astype(f32)).astype(bf16)
+        for r in range(rows):
+            kept[r, span, :] = total[:, r * width : (r + 1) * width]
+        z_copies.append(
+            [
+                remote(
+                    kept.at[others[step], span],
+                    landing.at[step, span],
+                    z_send.at[index, step],
+                    z_recv.at[index, step],
+                    row_ids[step],
+                )
+                for step in range(rows - 1)
+            ]
+        )
+
+    def z_stage(index):
+        which, b = pieces[index]
+        for copy in z_copies[index]:
+            copy.wait_recv()
+        lines = pl.ds(b * block, block)
+        if which is None:
+            kept, landing, span = kv_a2, kv_rz, pl.ds(0, block)
+        else:
+            kept, landing, span = a2s[which], rzs[which], lines
+        total = kept[row, span, :].astype(f32)
+        for step in range(rows - 1):
+            total = total + landing[step, span, :].astype(f32)
+        if which is None:
+            kv_own[...] = total
+            return [
+                remote(
+                    kv_own, kv_all.at[step], kv_send.at[step], kv_recv.at[step], plane_ids[step]
+                )
+                for step in range(3)
+            ]
+        outs[which][lines, :] = total.astype(outs[which].dtype)
+        return []
+
+    kv_copies = []
+    sq_copies = [sq_copy]
+    for turn in range(len(pieces) + 2):
+        if turn < len(pieces):
+            core_stage(turn)
+        if turn == 1:
+            sq_copies[0].wait_recv()
+            sq_send[0] = sq_part[...] + sq_recv[0]
+            sq_copies.append(
+                remote(sq_send.at[0], sq_recv.at[1], sq_ss.at[1], sq_rs.at[1], x_id)
+            )
+        if turn == 3:
+            sq_copies[1].wait_recv()
+            sq_send[1] = sq_send[0] + sq_recv[1]
+            for step in range(rows - 1):
+                sq_copies.append(
+                    remote(
+                        sq_send.at[1],
+                        sq_recv.at[2 + step],
+                        sq_ss.at[2 + step],
+                        sq_rs.at[2 + step],
+                        row_ids[step],
+                    )
+                )
+        if 1 <= turn <= len(pieces):
+            x_stage(turn - 1)
+        if turn >= 2:
+            kv_copies += z_stage(turn - 2)
+    total = sq_send[1]
+    for step in range(rows - 1):
+        sq_copies[2 + step].wait_recv()
+        total = total + sq_recv[2 + step]
+    sq_out[...] = total
+    own_slot = 2 * core + across
+    kv_out[pl.ds(pl.multiple_of(own_slot * block, block), block), :] = kv_own[...]
+    for step in range(3):
+        kv_copies[step].wait_recv()
+        first = pl.multiple_of(plane_slots[step] * block, block)
+        kv_out[pl.ds(first, block), :] = kv_all[step]
+    for copy in sum(core_copies, []) + x_copies + sum(z_copies, []) + kv_copies + sq_copies:
+        copy.wait_send()
+
+
+def reduce_shares(q_part, o_part, kv_part, sq_part, rows):
+    f32, bf16 = jnp.float32, jnp.bfloat16
+    seq_len, whole = q_part.shape
+    width = whole // (4 * rows)
+    block = seq_len // 4
+    dma = pltpu.SemaphoreType.DMA
+    twice = lambda *shape: [pltpu.VMEM(shape, bf16)] * 2
+    return pl.pallas_call(
+        reduce_kernel,
+        out_shape=(
+            jax.ShapeDtypeStruct((seq_len, width), f32),
+            jax.ShapeDtypeStruct((seq_len, width), bf16),
+            jax.ShapeDtypeStruct((seq_len, width), f32),
+            jax.ShapeDtypeStruct(sq_part.shape, f32),
+        ),
+        in_specs=[pl.BlockSpec(memory_space=pltpu.VMEM)] * 4,
+        out_specs=[pl.BlockSpec(memory_space=pltpu.VMEM)] * 4,
+        scratch_shapes=[
+            *twice(seq_len, whole // 2),
+            pltpu.VMEM((seq_len // 2, rows * width), bf16),
+            *twice(2, seq_len, rows * width),
+            pltpu.VMEM((seq_len // 2, rows * width), bf16),
+            *twice(seq_len, rows * width),
+            pltpu.VMEM((block, rows * width), bf16),
+            *twice(rows, seq_len, width),
+            pltpu.VMEM((rows, block, width), bf16),
+            *twice(rows - 1, seq_len, width),
+            pltpu.VMEM((rows - 1, block, width), bf16),
+            pltpu.VMEM((block, width), f32),
+            pltpu.VMEM((3, block, width), f32),
+            pltpu.VMEM((2, *sq_part.shape), f32),
+            pltpu.VMEM((1 + rows, *sq_part.shape), f32),
+            dma((9, rows)), dma((9, rows)), dma((9,)), dma((9,)),
+            dma((9, rows - 1)), dma((9, rows - 1)), dma((3,)), dma((3,)),
+            dma((1 + rows,)), dma((1 + rows,)),
+        ],
+        compiler_params=pltpu.CompilerParams(
+            collective_id=0, has_side_effects=True, vmem_limit_bytes=VMEM_BYTES
+        ),
+    )(q_part, o_part, kv_part, sq_part)
+
+
+def gather_kernel(
+    a_own, q_own, kv_part, cos_ref, sin_ref, dot_part,
+    a_all, q_all, kv_all, dot_out,
+    kv_recv_buf, dot_send, dot_recv,
+    z_send, z_recv, x_send, x_recv, core_send, core_recv,
+    r_send, r_recv, kz_send, kz_recv, kp_send, kp_recv, dot_ss, dot_rs,
+):
+    f32, bf16 = jnp.float32, jnp.bfloat16
+    row, across, core, plane_ids, plane_slots, others, row_ids = neighbours()
+    rows = len(others) + 1
+    core_id, x_id = plane_ids[0], plane_ids[1]
+    seq_len, width = a_own.shape
+    block = seq_len // 4
+    wide = 2 * width
+    own_slot = 2 * core + across
+    own_first = pl.multiple_of(row * 2 * wide + own_slot * width, width)
+    own_lines = pl.ds(pl.multiple_of(own_slot * block, block), block)
+    own_kv = pl.ds(pl.multiple_of(row * width, width), width)
+    greet(plane_ids + row_ids)
+
+    reduces = []
+    for step in range(3):
+        first = pl.multiple_of(plane_slots[step] * block, block)
+        reduces.append(
+            remote(
+                kv_part.at[pl.ds(first, block)],
+                kv_recv_buf.at[step],
+                r_send.at[step],
+                r_recv.at[step],
+                plane_ids[step],
+            )
+        )
+    dot_copies = [
+        remote(dot_part, dot_recv.at[step], dot_ss.at[step], dot_rs.at[step], row_ids[step])
+        for step in range(rows - 1)
+    ]
+    pieces = [(which, b) for which in range(2) for b in range(4)]
+    owns, alls = (a_own, q_own), (a_all, q_all)
+    z_copies, x_copies, core_copies = [], [], []
+    for index, (which, b) in enumerate(pieces):
+        lines = pl.ds(b * block, block)
+        z_copies.append(
+            [
+                remote(
+                    owns[which].at[lines],
+                    alls[which].at[lines, pl.ds(own_first, width)],
+                    z_send.at[index, step],
+                    z_recv.at[index, step],
+                    row_ids[step],
+                )
+                for step in range(rows - 1)
+            ]
+        )
+    for which in range(2):
+        alls[which][:, pl.ds(own_first, width)] = owns[which][...]
+
+    total = kv_part[own_lines, :].astype(f32)
+    for step in range(3):
+        reduces[step].wait_recv()
+        total = total + kv_recv_buf[step].astype(f32)
+    head = width // 2
+    key_part = total[:, :head]
+    cosines, sines = cos_ref[own_lines, :], sin_ref[own_lines, :]
+    turned = jnp.concatenate([key_part[:, head // 2 :], key_part[:, : head // 2]], axis=1)
+    key_part = key_part * cosines + turned * sines
+    kv_all[own_lines, own_kv] = jnp.concatenate([key_part, total[:, head:]], axis=1).astype(bf16)
+    kv_z = [
+        remote(
+            kv_all.at[own_lines, own_kv],
+            kv_all.at[own_lines, own_kv],
+            kz_send.at[step],
+            kz_recv.at[step],
+            row_ids[step],
+        )
+        for step in range(rows - 1)
+    ]
+
+    def x_stage(index):
+        which, b = pieces[index]
+        lines = pl.ds(b * block, block)
+        for copy in z_copies[index]:
+            copy.wait_recv()
+        copies = []
+        for r in range(rows):
+            first = pl.multiple_of(r * 2 * wide + own_slot * width, width)
+            place = alls[which].at[lines, pl.ds(first, width)]
+            copies.append(remote(place, place, x_send.at[index, r], x_recv.at[index, r], x_id))
+        x_copies.append(copies)
+
+    def core_stage(index):
+        which, b = pieces[index]
+        lines = pl.ds(b * block, block)
+        for copy in x_copies[index]:
+            copy.wait_recv()
+        copies = []
+        for r in range(rows):
+            first = pl.multiple_of(r * 2 * wide + core * wide, wide)
+            place = alls[which].at[lines, pl.ds(first, wide)]
+            copies.append(
+                remote(place, place, core_send.at[index, r], core_recv.at[index, r], core_id)
+            )
+        core_copies.append(copies)
+
+    kv_plane = []
+    for turn in range(len(pieces) + 1):
+        if turn < len(pieces):
+            x_stage(turn)
+        if turn == 0:
+            total = dot_part[...]
+            for step in range(rows - 1):
+                dot_copies[step].wait_recv()
+                total = total + dot_recv[step]
+            dot_send[0] = total
+            dot_copies.append(
+                remote(
+                    dot_send.at[0],
+                    dot_recv.at[rows - 1],
+                    dot_ss.at[rows - 1],
+                    dot_rs.at[rows - 1],
+                    x_id,
+                )
+            )
+        if turn == 1:
+            for copy in kv_z:
+                copy.wait_recv()
+            kv_plane = [
+                remote(
+                    kv_all.at[own_lines],
+                    kv_all.at[own_lines],
+                    kp_send.at[step],
+                    kp_recv.at[step],
+                    plane_ids[step],
+                )
+                for step in range(3)
+            ]
+        if turn == 2:
+            dot_copies[rows - 1].wait_recv()
+            dot_send[1] = dot_send[0] + dot_recv[rows - 1]
+            dot_copies.append(
+                remote(
+                    dot_send.at[1], dot_recv.at[rows], dot_ss.at[rows], dot_rs.at[rows], core_id
+                )
+            )
+        if turn >= 1:
+            core_stage(turn - 1)
+    dot_copies[rows].wait_recv()
+    dot_out[...] = dot_send[1] + dot_recv[rows]
+    for copy in kv_plane + sum(core_copies, []):
+        copy.wait_recv()
+    for copy in (
+        sum(z_copies + x_copies + core_copies, []) + reduces + kv_z + kv_plane + dot_copies
+    ):
+        copy.wait_send()
+
+
+def gather_shares(a_own, q_own, kv_part, cosines, sines, dot_part, rows):
+    f32, bf16 = jnp.float32, jnp.bfloat16
+    seq_len, width = a_own.shape
+    block = seq_len // 4
+    whole = width * 4 * rows
+    dma = pltpu.SemaphoreType.DMA
+    return pl.pallas_call(
+        gather_kernel,
+        out_shape=(
+            jax.ShapeDtypeStruct((seq_len, whole), bf16),
+            jax.ShapeDtypeStruct((seq_len, whole), bf16),
+            jax.ShapeDtypeStruct((seq_len, rows * width), bf16),
+            jax.ShapeDtypeStruct(dot_part.shape, f32),
+        ),
+        in_specs=[pl.BlockSpec(memory_space=pltpu.VMEM)] * 6,
+        out_specs=[pl.BlockSpec(memory_space=pltpu.VMEM)] * 4,
+        scratch_shapes=[
+            pltpu.VMEM((3, block, width), bf16),
+            pltpu.VMEM((2, *dot_part.shape), f32),
+            pltpu.VMEM((rows + 1, *dot_part.shape), f32),
+            dma((8, rows - 1)), dma((8, rows - 1)), dma((8, rows)), dma((8, rows)),
+            dma((8, rows)), dma((8, rows)), dma((3,)), dma((3,)),
+            dma((rows - 1,)), dma((rows - 1,)), dma((3,)), dma((3,)),
+            dma((rows + 1,)), dma((rows + 1,)),
+        ],
+        compiler_params=pltpu.CompilerParams(
+            collective_id=1, has_side_effects=True, vmem_limit_bytes=VMEM_BYTES
+        ),
+    )(a_own, q_own, kv_part, cosines, sines, dot_part)
+
+
 def fast_device(
     motion_ids,
     audio_ids,
@@ -292,15 +719,12 @@
     row_devices = lax.axis_size("row")
     seq_devices = lax.axis_size("seq")
     groups = row_devices * seq_devices
-    row_index = lax.axis_index("row")
-    seq_index = lax.axis_index("seq")
     col_index = lax.axis_index("col")
     own_len = out_grad.shape[0]
     model_width = out_grad.shape[1]
     query_width = w_query.shape[1]
     kv_width = w_key.shape[1]
     head_count = query_width // HD // groups
-    kv_len = seq_len // seq_devices
     score_scale = HD ** (-0.5)
 
     embedded = (
@@ -313,12 +737,13 @@
     embedded_all = both[:, :model_width]
     grad_all = both[:, model_width:]
     residual_all = embedded_all.astype(f32)
-    squares = lax.psum(jnp.sum(residual_all * residual_all, axis=1), ("row", "seq"))
-    inverse = lax.rsqrt(squares / D + epsilon)
     scaled = (residual_all * norm_gain[None, :]).astype(bf16)
 
     def product(left, right):
         return jnp.dot(left, right, preferred_element_type=f32).astype(bf16)
+
+    def as_rows(vector):
+        return jnp.broadcast_to(vector[None, :], (8, seq_len))
 
     kv_part = jnp.concatenate(
         [
@@ -327,16 +752,16 @@
         ],
         axis=2,
     ).reshape(seq_len, 2 * kv_width)
-    kv_sum = lax.psum(
-        lax.psum_scatter(kv_part, "row", scatter_dimension=1, tiled=True), "seq"
-    ).astype(f32)
-    query_sum = lax.psum_scatter(
-        product(scaled, w_query), ("row", "seq"), scatter_dimension=1, tiled=True
-    ).astype(f32)
     out_part = jnp.einsum("ld,nd->ln", grad_all, w_out, preferred_element_type=f32).astype(bf16)
-    out_heads = lax.psum_scatter(
-        out_part, ("row", "seq"), scatter_dimension=1, tiled=True
-    ).reshape(seq_len, head_count, HD)
+    query_sum, out_heads, kv_sum, squares = reduce_shares(
+        product(scaled, w_query),
+        out_part,
+        kv_part,
+        as_rows(jnp.sum(residual_all * residual_all, axis=1)),
+        row_devices,
+    )
+    inverse = lax.rsqrt(squares[0] / D + epsilon)
+    out_heads = out_heads.reshape(seq_len, head_count, HD)
 
     positions = jnp.arange(seq_len, dtype=jnp.int32)
     cosines, sines = rotary_tables(positions, HD)
@@ -358,8 +783,6 @@
         "hqk,kd->qhd", weights.astype(bf16), values, preferred_element_type=f32
     )
     attn_out = (attended / totals.T[:, :, None]).astype(bf16).reshape(seq_len, head_count * HD)
-    out_all = lax.all_gather(attn_out, ("row", "seq"), axis=1, tiled=True)
-
     probs = weights / totals[:, :, None]
     prob_grads = jnp.einsum("qhd,kd->hqk", out_heads, values, preferred_element_type=f32)
     row_dots = jnp.sum(probs * prob_grads, axis=2, keepdims=True)
@@ -375,32 +798,22 @@
     grad_query_own = (
         rotate_back(grad_query, cosines, sines).astype(bf16).reshape(seq_len, head_count * HD)
     )
-    kv_first = seq_index * kv_len
-    kv_grad = lax.psum_scatter(
+    dot_part = dot_query + jnp.sum(
+        grad_key * keys.astype(f32) + grad_value * values.astype(f32), axis=1
+    )
+    out_all, grad_query_all, kv_grad_all, dot_sum = gather_shares(
+        attn_out,
+        grad_query_own,
         jnp.concatenate([grad_key, grad_value], axis=1).astype(bf16),
-        "seq",
-        scatter_dimension=0,
-        tiled=True,
-    ).astype(f32)
-
-    def own_rows(array):
-        return lax.dynamic_slice_in_dim(array, kv_first, kv_len, axis=0)
-
-    kv_own = own_rows(jnp.concatenate([keys, values], axis=1)).astype(f32)
-    dot_kv = jnp.sum(kv_grad * kv_own, axis=1)
-    dot_part = lax.dynamic_update_slice_in_dim(
-        dot_query, own_rows(dot_query) + dot_kv, kv_first, axis=0
-    )
-    grad_key_own = rotate_back(kv_grad[:, None, :HD], own_rows(cosines), own_rows(sines))[:, 0]
-    kv_grad_own = jnp.concatenate([grad_key_own, kv_grad[:, HD:]], axis=1).astype(bf16)
-    kv_grad_all = lax.all_gather(
-        lax.all_gather(kv_grad_own, "seq", axis=0, tiled=True), "row", axis=1, tiled=False
-    )
-    grad_query_all = lax.all_gather(grad_query_own, ("row", "seq"), axis=1, tiled=True)
+        jnp.concatenate([cosines, cosines], axis=1),
+        jnp.concatenate([sines, -sines], axis=1),
+        as_rows(dot_part),
+        row_devices,
+    )
+    kv_grad_all = kv_grad_all.reshape(seq_len, row_devices, 2 * HD)
     grad_key_all = kv_grad_all[:, :, :HD].reshape(seq_len, kv_width)
     grad_value_all = kv_grad_all[:, :, HD:].reshape(seq_len, kv_width)
 
-    dot_sum = lax.psum(dot_part, ("row", "seq", "col"))
     normed = (residual_all * inverse[:, None] * norm_gain[None, :]).astype(bf16)
     branch_part = product(out_all, w_out)
     grad_wo = jnp.einsum("ln,ld->nd", out_all, grad_all, preferred_element_type=f32)
@@ -424,7 +837,8 @@
         .reshape(own_len, 2, model_width)
         .swapaxes(0, 1)
     )
-    grad_gain = lax.psum(gain_part, "col")
+    sums = lax.psum(jnp.concatenate([gain_part, dot_sum[0]]), "col")
+    grad_gain, dot_sum = sums[:model_width], sums[model_width:]
 
     def own_part(array):
         return lax.dynamic_slice_in_dim(array, col_index * own_len, own_len, axis=0)
@@ -457,7 +871,7 @@
     groups = mesh.shape["row"] * mesh.shape["seq"]
     heads_col = H // mesh.shape["col"]
     whole_heads = (
-        heads_col % groups == 0
+        heads_col == 2 * groups
         and KV // mesh.shape["col"] == mesh.shape["row"]
         and mesh.shape["seq"] == 4
     )

time: 352 us -> 259 us (0.74)
  Pallas kernels: 0 us -> 143 us
  waiting for transfers between devices: 129 us -> 0.02 us
  blocking collectives: 125 us -> 17.8 us
  other arithmetic: 12 us -> 18.5 us
  matrix products: 53.2 us -> 49.2 us
    pallas_call x0 -> x2, Pallas kernels: none -> 143 us  [the longest x1 82.7 us: gather_shares(): pl.pallas_call(gather_kernel, out_shape=(jax.ShapeDtypeStruct((seq_len, w...]
    reduce_scatter x3 -> x0, waiting for transfers between devices: 118 us -> none  [the longest x1 66.2 us: fast_device(): lax.psum_scatter(out_part, ('row', 'seq'), scatter_dimension=1, tiled=True)]
    psum x3 -> x1, blocking collectives: 77.6 us -> 4.95 us  [fast_device(): sums = lax.psum(jnp.concatenate([gain_part, dot_sum[0]]), 'col')]
    all_gather x2 -> x0, blocking collectives: 34.7 us -> none  [the longest x1 29.1 us: fast_device(): lax.all_gather(lax.all_gather(kv_grad_own, 'seq', axis=0, tiled=True), 'r...]
    unnamed x9 -> x1, waiting for transfers between devices: 10.1 us -> 0.02 us
    unnamed x48 -> x49, local copies, waits for them, and re-layouts: 7.17 us -> 3.84 us
  transfers between devices with their start and end apart: 8 -> 1, of which waited for: 5 -> 0; matrix products, arithmetic and copies ran while one was open for 15% -> 6% of each run, Pallas kernels for 0% -> 0%
where the time goes in v2:
time: 259 us
  Pallas kernels  143 us (55%)
  matrix products  49.2 us (19%)
  other arithmetic  18.5 us (7%)
  blocking collectives  17.8 us (7%)
  local copies, waits for them, and re-layouts  15.6 us (6%)
  between operations  14.4 us (6%)
    pallas_call x1, Pallas kernels, gather_shares(): pl.pallas_call(gather_kernel, out_shape=(jax.ShapeDtypeStruct((seq_len, w...  82.7 us
    pallas_call x1, Pallas kernels, reduce_shares(): pl.pallas_call(reduce_kernel, out_shape=(jax.ShapeDtypeStruct((seq_len, w...  60.3 us
    all_gather x1, blocking collectives, fast_device(): lax.all_gather(jnp.concatenate([embedded, out_grad], axis=1), 'col', axis...  12.9 us
    dot_general x4, matrix products, product(): return jnp.dot(left, right, preferred_element_type=f32).astype(bf16)  9.32 us
    dot_general x1, matrix products, fast_device(): jnp.einsum('ld,ln->dn', normed, grad_query_all, preferred_element_type=f32)  5.88 us
    dot_general x1, matrix products, fast_device(): jnp.einsum('ld,nd->ln', grad_all, w_out, preferred_element_type=f32)  5.83 us
    dot_general x1, matrix products, fast_device(): jnp.einsum('ln,ld->nd', out_all, grad_all, preferred_element_type=f32)  5.81 us
  transfers between devices with their start and end apart: 1, of which 0 were waited for; matrix products, arithmetic and copies ran while one was open for 6% of the time, Pallas kernels for 0%

profile of v2, /device:TPU:0, one launch (start us, length us, event | category | flops | bytes accessed | tf_op | source)
XLA Modules:
  0.0 258.6 jit_solution(6286460019550294351)
XLA Ops:
  7.2 0.5 multiply_power_fusion
  7.8 0.7 compare_select_fusion.1
  8.4 0.7 compare_select_fusion
  9.1 0.7 compare_and_fusion
  9.8 0.6 iota_convert_fusion
  10.4 0.9 fusion.31
  11.3 2.2 gather_fusion
  13.5 1.0 gather_fusion.1
  14.7 12.9 %all_gather.3 = bf16[384,1024]{1,0:T(8,128)(2,1)S(1)} all-gather(bf16[192,1024]{1,0:T(8,128)(2,1)S(1)} %pad_maximum_fusion.2), channel_id=1, replica_groups=mesh['row'=4,'col'=2,'seq'=4] {'col'}, dimensions={0}, use_global_device_ids=true | all-gather | bytes 1179648 | tf_op jit(solution)/shard_map/all_gather | solution.py:734
  28.3 0.5 copy-done.6
  29.7 1.0 copy.79
  30.8 5.8 %convolution_convert_fusion.o_part = bf16[384,4096]{1,0:T(8,128)(2,1)} fusion(bf16[4096,512]{1,0:T(8,128)(2,1)} %param.20, bf16[384,1024]{1,0:T(8,128)(2,1)S(1)} %all_gather.3), kind=kOutput, calls=%fused_computation.3 | convolution fusion | flops 1612185600 | bytes 7733248 | tf_op jit(solution)/shard_map/ld,nd->ln/dot_general | solution.py:755
  36.6 3.5 %convolution_convert_fusion.1.q_part = bf16[384,4096]{1,0:T(8,128)(2,1)} fusion(bf16[512,4096]{1,0:T(8,128)(2,1)S(1)} %copy-done.20, f32[512]{0:T(512)S(1)} %copy-done.16, bf16[384,1024]{1,0:T(8,128)(2,1)S(1)} %all_gather.3), kind=kOutput, calls=%fused_computation.4 | convolution fusion | flops 1612775424 | bytes 7735296 | tf_op jit(solution)/shard_map/dot_general | solution.py:743
  40.1 0.6 broadcast_in_dim.45.sq_part
  40.7 60.3 %shard_map.162 = (f32[384,256]{1,0:T(8,128)}, bf16[384,256]{1,0:T(8,128)(2,1)}, f32[384,256]{1,0:T(8,128)}, f32[8,384]{1,0:T(8,128)}) custom-call(bf16[384,4096]{1,0:T(8,128)(2,1)} %convolution_convert_fusion.1.q_part, bf16[384,4096]{1,0:T(8,128)(2,1)} %convolution_convert_fusion.o_part, bf16[384,1024]{1,0:T(8,128)(2,1)} %bitcast.144, ...), custom_call_target="tpu_custom_call" | custom-call | tf_op jit(solution)/shard_map/pallas_call | solution.py:483
  101.0 1.3 fusion.88
  102.3 1.2 broadcast_multiply_fusion
  103.8 2.1 fusion.70
  106.0 2.2 fusion.60
  108.2 1.1 copy.76
  109.3 0.5 fusion.90
  109.7 1.3 convolution_bitcast_fusion
  111.2 0.8 copy-done.12
  112.0 2.2 fusion.21
  114.2 4.2 %convolution_bitcast_fusion.4 = f32[384,128]{1,0:T(8,128)} fusion(f32[2,384,384]{1,2,0:T(8,128)} %convolution_bitcast_fusion, f32[384,384,2]{1,0,2:T(8,128)} %get-tuple-element.48, bf16[384,2,64]{2,0,1:T(8,128)(2,1)S(1)} %get-tuple-element.26, bf16[384,2,64]{2,0,1:T(8,128)(2,1)S(1)} %get-tuple-element.25, f32[2,384]{1,0:T(2,128)} %get-tuple-element.47, ...), kind=kOutput, calls=%fused_computation.28 | convolution fusion | flops 80020608 | bytes 2903040 | tf_op jit(solution)/shard_map/hqk,qhd->kd/dot_general | solution.py:793
  118.4 4.6 %multiply_reduce_fusion.1 = (f32[384]{0:T(512)}, f32[384,2,128]{2,0,1:T(8,128)S(1)}) fusion(bf16[384,2,64]{2,0,1:T(8,128)(2,1)} %copy-done.11, bf16[384,2,64]{2,0,1:T(8,128)(2,1)} %copy-done.10, f32[2,384,384]{1,2,0:T(8,128)} %convolution_bitcast_fusion, f32[384,384,2]{1,0,2:T(8,128)} %get-tuple-element.48, f32[2,384]{1,0:T(2,128)} %get-tuple-element.47, ...), kind=kOutput, calls=%fused_computation.70 | convolution fusion | flops 80413440 | bytes 3199488 | tf_op jit(solution)/shard_map/hqk,kd->qhd/dot_general | solution.py:792
  123.0 1.8 pad_maximum_fusion.5
  124.8 2.4 fusion.8
  127.2 1.7 copy.68.a_own
  128.9 1.9 add_reduce_fusion
  131.5 0.8 copy_bitcast_fusion.q_own
  132.3 0.7 pad_maximum_fusion.4.kv_part
  133.0 0.6 broadcast_in_dim.49.dot_part
  133.6 82.7 %shard_map.163 = (bf16[384,4096]{1,0:T(8,128)(2,1)}, bf16[384,4096]{1,0:T(8,128)(2,1)}, bf16[384,1024]{1,0:T(8,128)(2,1)}, f32[8,384]{1,0:T(8,128)}) custom-call(bf16[384,256]{1,0:T(8,128)(2,1)} %copy.68.a_own, bf16[384,256]{1,0:T(8,128)(2,1)} %copy_bitcast_fusion.q_own, bf16[384,256]{1,0:T(8,128)(2,1)} %pad_maximum_fusion.4.kv_part, ...), custom_call_target="tpu_custom_call" | custom-call | tf_op jit(solution)/shard_map/pallas_call | solution.py:679
  216.4 2.0 reshape.237
  218.7 5.1 %convolution_convert_fusion.4 = bf16[384,512]{1,0:T(8,128)(2,1)S(1)} fusion(bf16[384,4096]{1,0:T(8,128)(2,1)} %get-tuple-element.19, bf16[4096,512]{1,0:T(8,128)(2,1)} %param.20), kind=kOutput, calls=%fused_computation.21 | convolution fusion | flops 1610809344 | bytes 7733248 | tf_op jit(solution)/shard_map/dot_general | solution.py:743
  224.0 1.8 fusion.93
  226.9 0.5 fusion.17
  227.4 1.0 pad_maximum_fusion.1
  228.5 0.7 slice_reduce_fusion
  229.2 4.9 %psum.7 = f32[896]{0:T(1024)S(1)} all-reduce(f32[896]{0:T(1024)S(1)} %pad_maximum_fusion.8), channel_id=1, replica_groups=mesh['row'=4,'col'=2,'seq'=4] {'col'}, use_global_device_ids=true, to_apply=%region_7.8 | all-reduce | flops 896 | bytes 7168 | tf_op jit(solution)/shard_map/psum | solution.py:840
  234.2 0.6 slice.64
  234.9 1.5 fusion.36
  236.4 1.5 fusion.39
  238.0 5.8 %fusion.49 = f32[4096,512]{1,0:T(8,128)} fusion(bf16[384,4096]{1,0:T(8,128)(2,1)S(1)} %copy-done.1, bf16[384,1024]{1,0:T(8,128)(2,1)S(1)} %all_gather.3), kind=kOutput, calls=%fused_computation.80 | convolution fusion | flops 1610612736 | bytes 11927552 | tf_op jit(solution)/shard_map/ln,ld->nd/dot_general | solution.py:819
  243.8 5.9 %fusion.81 = f32[512,4096]{1,0:T(8,128)} fusion(bf16[384,4096]{1,0:T(8,128)(2,1)S(1)} %copy-done.3, f32[384]{0:T(512)S(1)} %copy-done.15, f32[512]{0:T(512)S(1)} %copy-done.17, bf16[384,1024]{1,0:T(8,128)(2,1)S(1)} %all_gather.3), kind=kOutput, calls=%fused_computation.136 | convolution fusion | flops 1611399168 | bytes 11931648 | tf_op jit(solution)/shard_map/ld,ln->dn/dot_general | solution.py:820
  249.7 1.1 transpose.70
  250.9 0.9 fusion.35
  (71 shorter events, 4.7 us)
Async XLA Ops:
  7.2 6.3 %copy-start = (bf16[1024,512]{1,0:T(8,128)(2,1)S(1)}, bf16[1024,512]{1,0:T(8,128)(2,1)}, u32[]{:S(2)}) copy-start(bf16[1024,512]{1,0:T(8,128)(2,1)} %param.15) | copy-start | bytes 3145732
  7.2 242.5 %reduce-scatter.2.cloned.1.call-start = ((), (), s32[]{:S(2)}) async-start(), calls=%async_computation.1 | async-start | bytes 1179648 | tf_op jit(solution)/shard_map/reduce_scatter | solution.py:830
  13.5 1.2 copy-start.4
  14.7 13.1 %copy-start.16 = (f32[512]{0:T(512)S(1)}, f32[512]{0:T(512)}, u32[]{:S(2)}) copy-start(f32[512]{0:T(512)} %param.16) | copy-start | bytes 6148
  14.7 13.1 %copy-start.22 = (bf16[512,512]{1,0:T(8,128)(2,1)S(1)}, bf16[512,512]{1,0:T(8,128)(2,1)}, u32[]{:S(2)}) copy-start(bf16[512,512]{1,0:T(8,128)(2,1)} %param.19) | copy-start | bytes 1572868
  27.8 1.0 copy-start.6
  30.8 5.8 %copy-start.20 = (bf16[512,4096]{1,0:T(8,128)(2,1)S(1)}, bf16[512,4096]{1,0:T(8,128)(2,1)}, u32[]{:S(2)}) copy-start(bf16[512,4096]{1,0:T(8,128)(2,1)} %param.17) | copy-start | bytes 12582916
  102.3 1.5 copy-start.14
  111.1 0.9 copy-start.12
  111.1 0.9 copy-start.13
  111.2 3.0 %copy-start.10 = (bf16[384,2,64]{2,0,1:T(8,128)(2,1)}, bf16[384,2,64]{2,0,1:T(8,128)(2,1)S(1)}, u32[]{:S(2)}) copy-start(bf16[384,2,64]{2,0,1:T(8,128)(2,1)S(1)} %get-tuple-element.25) | copy-start | bytes 294916
  111.2 3.0 %copy-start.11 = (bf16[384,2,64]{2,0,1:T(8,128)(2,1)}, bf16[384,2,64]{2,0,1:T(8,128)(2,1)S(1)}, u32[]{:S(2)}) copy-start(bf16[384,2,64]{2,0,1:T(8,128)(2,1)S(1)} %get-tuple-element.26) | copy-start | bytes 294916
  130.9 0.7 copy-start.19
  218.6 7.7 %copy-start.8 = (bf16[384,4,128]{2,1,0:T(4,128)(2,1)}, bf16[384,4,128]{2,1,0:T(4,128)(2,1)S(1)}, u32[]{:S(2)}) copy-start(bf16[384,4,128]{2,1,0:T(4,128)(2,1)S(1)} %get-tuple-element.31) | copy-start | bytes 1179652
  218.6 5.1 %copy-start.2 = (bf16[384,4096]{1,0:T(8,128)(2,1)S(1)}, bf16[384,4096]{1,0:T(8,128)(2,1)}, u32[]{:S(2)}) copy-start(bf16[384,4096]{1,0:T(8,128)(2,1)} %get-tuple-element.20) | copy-start | bytes 9437188
  218.6 5.4 %copy-start.21 = (bf16[512,4096]{1,0:T(8,128)(2,1)S(1)}, bf16[512,4096]{1,0:T(8,128)(2,1)}, u32[]{:S(2)}) copy-start(bf16[512,4096]{1,0:T(8,128)(2,1)} %param.17) | copy-start | bytes 12582916
  224.0 1.8 copy-start.7
  225.9 0.7 copy-start.15
  225.9 1.0 copy-start.23
  227.4 7.4 %copy-start.18 = (f32[1,384]{1,0:T(1,128)S(1)}, f32[1,384]{1,0:T(1,128)}, u32[]{:S(2)}) copy-start(f32[1,384]{1,0:T(1,128)} %get-tuple-element.24) | copy-start | bytes 4612
  227.4 7.5 %copy-start.9 = (bf16[384,4,128]{2,1,0:T(4,128)(2,1)S(1)}, bf16[384,4,128]{2,1,0:T(4,128)(2,1)}, u32[]{:S(2)}) copy-start(bf16[384,4,128]{2,1,0:T(4,128)(2,1)} %copy-done.8) | copy-start | bytes 1179652
  227.4 7.5 %copy-start.17 = (f32[512]{0:T(512)S(1)}, f32[512]{0:T(512)}, u32[]{:S(2)}) copy-start(f32[512]{0:T(512)} %param.16) | copy-start | bytes 6148
  234.9 3.1 %copy-start.1 = (bf16[384,4096]{1,0:T(8,128)(2,1)S(1)}, bf16[384,4096]{1,0:T(8,128)(2,1)}, u32[]{:S(2)}) copy-start(bf16[384,4096]{1,0:T(8,128)(2,1)} %get-tuple-element.19) | copy-start | bytes 9437188
  238.0 5.8 %copy-start.3 = (bf16[384,4096]{1,0:T(8,128)(2,1)S(1)}, bf16[384,4096]{1,0:T(8,128)(2,1)}, u32[]{:S(2)}) copy-start(bf16[384,4096]{1,0:T(8,128)(2,1)} %get-tuple-element.20) | copy-start | bytes 9437188
  249.7 1.2 copy-start.5
Sparse Core Ops, SparseCore 0:
  228.6 18.7 reduce-scatter.1

commit v3 on v2

--- a/solution.py
+++ b/solution.py
@@ -337,7 +337,9 @@
     core_copies, x_copies, z_copies = [], [], []
 
     sq_copy = remote(sq_part, sq_recv.at[0], sq_ss.at[0], sq_rs.at[0], core_id)
-    for index, (which, b) in enumerate(pieces):
+
+    def start_core(index):
+        which, b = pieces[index]
         copies = []
         if which is None:
             source = kv_part.at[pl.ds(pl.multiple_of((1 - core) * half_len, half_len), half_len)]
@@ -359,10 +361,15 @@
                 )
         core_copies.append(copies)
 
+    for index in range(3):
+        start_core(index)
+
     def core_stage(index):
         which, b = pieces[index]
         for copy in core_copies[index]:
             copy.wait_recv()
+        if index + 3 < len(pieces):
+            start_core(index + 3)
         if which is None:
             own = kv_part[pl.ds(pl.multiple_of(core * half_len, half_len), half_len), :]
             kv_a1[...] = (own.astype(f32) + kv_rc[...].astype(f32)).astype(bf16)
@@ -432,7 +439,7 @@
 
     kv_copies = []
     sq_copies = [sq_copy]
-    for turn in range(len(pieces) + 2):
+    for turn in range(len(pieces) + 5):
         if turn < len(pieces):
             core_stage(turn)
         if turn == 1:
@@ -454,10 +461,10 @@
                         row_ids[step],
                     )
                 )
-        if 1 <= turn <= len(pieces):
-            x_stage(turn - 1)
-        if turn >= 2:
-            kv_copies += z_stage(turn - 2)
+        if 2 <= turn <= len(pieces) + 1:
+            x_stage(turn - 2)
+        if turn >= 5:
+            kv_copies += z_stage(turn - 5)
     total = sq_send[1]
     for step in range(rows - 1):
         sq_copies[2 + step].wait_recv()
@@ -516,8 +523,9 @@
 
 
 def gather_kernel(
-    a_own, q_own, kv_part, cos_ref, sin_ref, dot_part,
+    q_sum, o_heads, kv_sum, squares, mask, cos_ref, sin_ref,
     a_all, q_all, kv_all, dot_out,
+    a_own, q_own, kv_part, q_heads, probs, tanhs, dot_part,
     kv_recv_buf, dot_send, dot_recv,
     z_send, z_recv, x_send, x_recv, core_send, core_recv,
     r_send, r_recv, kz_send, kz_recv, kp_send, kp_recv, dot_ss, dot_rs,
@@ -529,11 +537,84 @@
     seq_len, width = a_own.shape
     block = seq_len // 4
     wide = 2 * width
+    head = width // 2
     own_slot = 2 * core + across
     own_first = pl.multiple_of(row * 2 * wide + own_slot * width, width)
     own_lines = pl.ds(pl.multiple_of(own_slot * block, block), block)
     own_kv = pl.ds(pl.multiple_of(row * width, width), width)
     greet(plane_ids + row_ids)
+
+    def swapped(values):
+        return jnp.concatenate([values[:, head // 2 :], values[:, : head // 2]], axis=1)
+
+    def dot(left, right, dims):
+        return lax.dot_general(left, right, ((dims[:1], dims[1:]), ((), ())), preferred_element_type=f32)
+
+    score_scale = HD ** (-0.5)
+    inverse = jnp.broadcast_to(lax.rsqrt(squares[0:1, :] / D + epsilon), (head, seq_len)).T
+    key_raw = kv_sum[:, :head] * inverse
+    keys = (key_raw * cos_ref[...] + swapped(key_raw) * sin_ref[...]).astype(bf16)
+    values = (kv_sum[:, head:] * inverse).astype(bf16)
+    for h in range(2):
+        lanes = pl.ds(h * head, head)
+        raw = q_sum[:, lanes] * inverse
+        query = (raw * cos_ref[...] + swapped(raw) * sin_ref[...]).astype(bf16)
+        q_heads[:, lanes] = query
+        tanh_scores = jnp.tanh(dot(query, keys, (1, 1)) * (score_scale / softcap))
+        weights = jnp.exp(softcap * tanh_scores) * mask[...]
+        totals = jnp.sum(weights, axis=1, keepdims=True)
+        attended = dot(weights.astype(bf16), values, (1, 0))
+        a_own[:, lanes] = (attended / totals).astype(bf16)
+        probs[h] = weights / totals
+        tanhs[h] = tanh_scores
+
+    pieces = [(which, b) for which in range(2) for b in range(4)]
+    owns, alls = (a_own, q_own), (a_all, q_all)
+    z_copies, x_copies, core_copies = [], [], []
+
+    def start_z(index):
+        which, b = pieces[index]
+        lines = pl.ds(b * block, block)
+        z_copies.append(
+            [
+                remote(
+                    owns[which].at[lines],
+                    alls[which].at[lines, pl.ds(own_first, width)],
+                    z_send.at[index, step],
+                    z_recv.at[index, step],
+                    row_ids[step],
+                )
+                for step in range(rows - 1)
+            ]
+        )
+
+    for index in range(3):
+        start_z(index)
+    a_all[:, pl.ds(own_first, width)] = a_own[...]
+
+    dots = jnp.zeros((seq_len, head), f32)
+    grad_key = jnp.zeros((seq_len, head), f32)
+    grad_value = jnp.zeros((seq_len, head), f32)
+    for h in range(2):
+        lanes = pl.ds(h * head, head)
+        out_head, query, prob = o_heads[:, lanes], q_heads[:, lanes], probs[h]
+        prob_grads = dot(out_head, values, (1, 1))
+        row_dots = jnp.sum(prob * prob_grads, axis=1, keepdims=True)
+        grad_scores = (
+            prob * (prob_grads - row_dots) * (1.0 - tanhs[h] * tanhs[h]) * score_scale
+        ).astype(bf16)
+        grad_query = dot(grad_scores, keys, (1, 0))
+        grad_key = grad_key + dot(grad_scores, query, (0, 0))
+        grad_value = grad_value + dot(prob.astype(bf16), out_head, (0, 0))
+        dots = dots + grad_query * query.astype(f32)
+        q_own[:, lanes] = (
+            grad_query * cos_ref[...] - swapped(grad_query) * sin_ref[...]
+        ).astype(bf16)
+    dots = dots + grad_key * keys.astype(f32) + grad_value * values.astype(f32)
+    dot_part[...] = jnp.broadcast_to(jnp.sum(dots.T, axis=0, keepdims=True), dot_part.shape)
+    kv_part[:, :head] = grad_key.astype(bf16)
+    kv_part[:, head:] = grad_value.astype(bf16)
+    q_all[:, pl.ds(own_first, width)] = q_own[...]
 
     reduces = []
     for step in range(3):
@@ -551,52 +632,34 @@
         remote(dot_part, dot_recv.at[step], dot_ss.at[step], dot_rs.at[step], row_ids[step])
         for step in range(rows - 1)
     ]
-    pieces = [(which, b) for which in range(2) for b in range(4)]
-    owns, alls = (a_own, q_own), (a_all, q_all)
-    z_copies, x_copies, core_copies = [], [], []
-    for index, (which, b) in enumerate(pieces):
-        lines = pl.ds(b * block, block)
-        z_copies.append(
-            [
-                remote(
-                    owns[which].at[lines],
-                    alls[which].at[lines, pl.ds(own_first, width)],
-                    z_send.at[index, step],
-                    z_recv.at[index, step],
-                    row_ids[step],
-                )
-                for step in range(rows - 1)
-            ]
+    def finish_kv():
+        total = kv_part[own_lines, :].astype(f32)
+        for step in range(3):
+            reduces[step].wait_recv()
+            total = total + kv_recv_buf[step].astype(f32)
+        key_part = total[:, :head]
+        key_part = key_part * cos_ref[own_lines, :] - swapped(key_part) * sin_ref[own_lines, :]
+        kv_all[own_lines, own_kv] = jnp.concatenate([key_part, total[:, head:]], axis=1).astype(
+            bf16
         )
-    for which in range(2):
-        alls[which][:, pl.ds(own_first, width)] = owns[which][...]
-
-    total = kv_part[own_lines, :].astype(f32)
-    for step in range(3):
-        reduces[step].wait_recv()
-        total = total + kv_recv_buf[step].astype(f32)
-    head = width // 2
-    key_part = total[:, :head]
-    cosines, sines = cos_ref[own_lines, :], sin_ref[own_lines, :]
-    turned = jnp.concatenate([key_part[:, head // 2 :], key_part[:, : head // 2]], axis=1)
-    key_part = key_part * cosines + turned * sines
-    kv_all[own_lines, own_kv] = jnp.concatenate([key_part, total[:, head:]], axis=1).astype(bf16)
-    kv_z = [
-        remote(
-            kv_all.at[own_lines, own_kv],
-            kv_all.at[own_lines, own_kv],
-            kz_send.at[step],
-            kz_recv.at[step],
-            row_ids[step],
-        )
-        for step in range(rows - 1)
-    ]
+        return [
+            remote(
+                kv_all.at[own_lines, own_kv],
+                kv_all.at[own_lines, own_kv],
+                kz_send.at[step],
+                kz_recv.at[step],
+                row_ids[step],
+            )
+            for step in range(rows - 1)
+        ]
 
     def x_stage(index):
         which, b = pieces[index]
         lines = pl.ds(b * block, block)
         for copy in z_copies[index]:
             copy.wait_recv()
+        if index + 3 < len(pieces):
+            start_z(index + 3)
         copies = []
         for r in range(rows):
             first = pl.multiple_of(r * 2 * wide + own_slot * width, width)
@@ -619,7 +682,7 @@
         core_copies.append(copies)
 
     kv_plane = []
-    for turn in range(len(pieces) + 1):
+    for turn in range(len(pieces) + 2):
         if turn < len(pieces):
             x_stage(turn)
         if turn == 0:
@@ -638,6 +701,8 @@
                 )
             )
         if turn == 1:
+            kv_z = finish_kv()
+        if turn == 4:
             for copy in kv_z:
                 copy.wait_recv()
             kv_plane = [
@@ -658,8 +723,8 @@
                     dot_send.at[1], dot_recv.at[rows], dot_ss.at[rows], dot_rs.at[rows], core_id
                 )
             )
-        if turn >= 1:
-            core_stage(turn - 1)
+        if turn >= 2:
+            core_stage(turn - 2)
     dot_copies[rows].wait_recv()
     dot_out[...] = dot_send[1] + dot_recv[rows]
     for copy in kv_plane + sum(core_copies, []):
@@ -670,9 +735,9 @@
         copy.wait_send()
 
 
-def gather_shares(a_own, q_own, kv_part, cosines, sines, dot_part, rows):
+def attend_and_gather(q_sum, o_heads, kv_sum, squares, mask, cosines, sines, rows):
     f32, bf16 = jnp.float32, jnp.bfloat16
-    seq_len, width = a_own.shape
+    seq_len, width = q_sum.shape
     block = seq_len // 4
     whole = width * 4 * rows
     dma = pltpu.SemaphoreType.DMA
@@ -682,14 +747,17 @@
             jax.ShapeDtypeStruct((seq_len, whole), bf16),
             jax.ShapeDtypeStruct((seq_len, whole), bf16),
             jax.ShapeDtypeStruct((seq_len, rows * width), bf16),
-            jax.ShapeDtypeStruct(dot_part.shape, f32),
+            jax.ShapeDtypeStruct(squares.shape, f32),
         ),
-        in_specs=[pl.BlockSpec(memory_space=pltpu.VMEM)] * 6,
+        in_specs=[pl.BlockSpec(memory_space=pltpu.VMEM)] * 7,
         out_specs=[pl.BlockSpec(memory_space=pltpu.VMEM)] * 4,
         scratch_shapes=[
+            *[pltpu.VMEM((seq_len, width), bf16)] * 4,
+            *[pltpu.VMEM((2, seq_len, seq_len), f32)] * 2,
+            pltpu.VMEM(squares.shape, f32),
             pltpu.VMEM((3, block, width), bf16),
-            pltpu.VMEM((2, *dot_part.shape), f32),
-            pltpu.VMEM((rows + 1, *dot_part.shape), f32),
+            pltpu.VMEM((2, *squares.shape), f32),
+            pltpu.VMEM((rows + 1, *squares.shape), f32),
             dma((8, rows - 1)), dma((8, rows - 1)), dma((8, rows)), dma((8, rows)),
             dma((8, rows)), dma((8, rows)), dma((3,)), dma((3,)),
             dma((rows - 1,)), dma((rows - 1,)), dma((3,)), dma((3,)),
@@ -698,7 +766,7 @@
         compiler_params=pltpu.CompilerParams(
             collective_id=1, has_side_effects=True, vmem_limit_bytes=VMEM_BYTES
         ),
-    )(a_own, q_own, kv_part, cosines, sines, dot_part)
+    )(q_sum, o_heads, kv_sum, squares, mask, cosines, sines)
 
 
 def fast_device(
@@ -717,19 +785,14 @@
     f32, bf16 = jnp.float32, jnp.bfloat16
     seq_len = segment_ids.shape[0]
     row_devices = lax.axis_size("row")
-    seq_devices = lax.axis_size("seq")
-    groups = row_devices * seq_devices
     col_index = lax.axis_index("col")
     own_len = out_grad.shape[0]
     model_width = out_grad.shape[1]
-    query_width = w_query.shape[1]
     kv_width = w_key.shape[1]
-    head_count = query_width // HD // groups
-    score_scale = HD ** (-0.5)
 
     embedded = (
-        jnp.take(motion_table, motion_ids, axis=0).astype(f32)
-        + jnp.take(audio_table, audio_ids, axis=0).astype(f32)
+        motion_table.at[motion_ids].get(mode="promise_in_bounds").astype(f32)
+        + audio_table.at[audio_ids].get(mode="promise_in_bounds").astype(f32)
     ).astype(bf16)
     both = lax.all_gather(
         jnp.concatenate([embedded, out_grad], axis=1), "col", axis=0, tiled=True
@@ -761,53 +824,19 @@
         row_devices,
     )
     inverse = lax.rsqrt(squares[0] / D + epsilon)
-    out_heads = out_heads.reshape(seq_len, head_count, HD)
-
     positions = jnp.arange(seq_len, dtype=jnp.int32)
     cosines, sines = rotary_tables(positions, HD)
-    query_heads = rotate_pairs(
-        (query_sum * inverse[:, None]).reshape(seq_len, head_count, HD), cosines, sines
-    ).astype(bf16)
-    kv_scaled = kv_sum * inverse[:, None]
-    keys = rotate_pairs(kv_scaled[:, None, :HD], cosines, sines)[:, 0].astype(bf16)
-    values = kv_scaled[:, HD:].astype(bf16)
-
     allowed = (positions[None, :] <= positions[:, None]) & (
         segment_ids[None, :] == segment_ids[:, None]
     )
-    raw_scores = jnp.einsum("qhd,kd->hqk", query_heads, keys, preferred_element_type=f32)
-    tanh_scores = jnp.tanh(raw_scores * (score_scale / softcap))
-    weights = jnp.where(allowed[None], jnp.exp(softcap * tanh_scores), 0.0)
-    totals = jnp.sum(weights, axis=2)
-    attended = jnp.einsum(
-        "hqk,kd->qhd", weights.astype(bf16), values, preferred_element_type=f32
-    )
-    attn_out = (attended / totals.T[:, :, None]).astype(bf16).reshape(seq_len, head_count * HD)
-    probs = weights / totals[:, :, None]
-    prob_grads = jnp.einsum("qhd,kd->hqk", out_heads, values, preferred_element_type=f32)
-    row_dots = jnp.sum(probs * prob_grads, axis=2, keepdims=True)
-    grad_scores = (
-        probs * (prob_grads - row_dots) * (1.0 - tanh_scores**2) * score_scale
-    ).astype(bf16)
-    grad_query = jnp.einsum("hqk,kd->qhd", grad_scores, keys, preferred_element_type=f32)
-    grad_key = jnp.einsum("hqk,qhd->kd", grad_scores, query_heads, preferred_element_type=f32)
-    grad_value = jnp.einsum(
-        "hqk,qhd->kd", probs.astype(bf16), out_heads, preferred_element_type=f32
-    )
-    dot_query = jnp.sum(grad_query * query_heads.astype(f32), axis=(1, 2))
-    grad_query_own = (
-        rotate_back(grad_query, cosines, sines).astype(bf16).reshape(seq_len, head_count * HD)
-    )
-    dot_part = dot_query + jnp.sum(
-        grad_key * keys.astype(f32) + grad_value * values.astype(f32), axis=1
-    )
-    out_all, grad_query_all, kv_grad_all, dot_sum = gather_shares(
-        attn_out,
-        grad_query_own,
-        jnp.concatenate([grad_key, grad_value], axis=1).astype(bf16),
+    out_all, grad_query_all, kv_grad_all, dot_sum = attend_and_gather(
+        query_sum,
+        out_heads,
+        kv_sum,
+        squares,
+        allowed.astype(f32),
         jnp.concatenate([cosines, cosines], axis=1),
-        jnp.concatenate([sines, -sines], axis=1),
-        as_rows(dot_part),
+        jnp.concatenate([-sines, sines], axis=1),
         row_devices,
     )
     kv_grad_all = kv_grad_all.reshape(seq_len, row_devices, 2 * HD)

time: 259 us -> 213 us (0.82)
  Pallas kernels: 143 us -> 127 us
  matrix products: 49.2 us -> 34.8 us
  other arithmetic: 18.5 us -> 8.96 us
  local copies, waits for them, and re-layouts: 15.6 us -> 9.2 us
    dot_general x6 -> x0, matrix products: 16.6 us -> none  [the longest x1 4.6 us: fast_device(): jnp.einsum('hqk,kd->qhd', grad_scores, keys, preferred_element_type=f32)]
    pallas_call x1, Pallas kernels: 82.7 us -> 67.2 us  [attend_and_gather(): pl.pallas_call(gather_kernel, out_shape=(jax.ShapeDtypeStruct((seq_len, w...]
    reshape x3 -> x0, local copies, waits for them, and re-layouts: 3.03 us -> none  [the longest x1 1.74 us: fast_device(): (attended / totals.T[:, :, None]).astype(bf16)]
  transfers between devices with their start and end apart: 1 -> 1, of which waited for: 0 -> 0; matrix products, arithmetic and copies ran while one was open for 6% -> 8% of each run, Pallas kernels for 0% -> 0%
where the time goes in v3:
time: 213 us; the launch traced here: 212 us
  Pallas kernels  127 us (60%)
  matrix products  34.8 us (16%)
  blocking collectives  17.7 us (8%)
  between operations  14.3 us (7%)
  local copies, waits for them, and re-layouts  9.2 us (4%)
  other arithmetic  8.96 us (4%)
    pallas_call x1, Pallas kernels, attend_and_gather(): pl.pallas_call(gather_kernel, out_shape=(jax.ShapeDtypeStruct((seq_len, w...  67.2 us
    pallas_call x1, Pallas kernels, reduce_shares(): pl.pallas_call(reduce_kernel, out_shape=(jax.ShapeDtypeStruct((seq_len, w...  60 us
    all_gather x1, blocking collectives, fast_device(): lax.all_gather(jnp.concatenate([embedded, out_grad], axis=1), 'col', axis...  12.8 us
    dot_general x4, matrix products, product(): return jnp.dot(left, right, preferred_element_type=f32).astype(bf16)  10.4 us
    dot_general x1, matrix products, fast_device(): jnp.einsum('ld,ln->dn', normed, grad_query_all, preferred_element_type=f32)  5.88 us
    dot_general x1, matrix products, fast_device(): jnp.einsum('ld,nd->ln', grad_all, w_out, preferred_element_type=f32)  5.83 us
    dot_general x1, matrix products, fast_device(): jnp.einsum('ln,ld->nd', out_all, grad_all, preferred_element_type=f32)  5.81 us
    psum x1, blocking collectives, fast_device(): sums = lax.psum(jnp.concatenate([gain_part, dot_sum[0]]), 'col')  4.95 us
  transfers between devices with their start and end apart: 1, of which 0 were waited for; matrix products, arithmetic and copies ran while one was open for 8% of the time, Pallas kernels for 0%

profile of v3, /device:TPU:0, one launch (start us, length us, event | category | flops | bytes accessed | tf_op | source)
XLA Modules:
  0.0 212.2 jit_solution(3510991978719827418)
XLA Ops:
  7.2 0.0 copy-start
  7.2 0.0 reduce-scatter.2.cloned.1.call-start
  7.2 0.5 multiply_power_fusion
  7.8 0.7 compare_select_fusion.1
  8.4 0.7 compare_select_fusion
  9.2 2.2 %gather_fusion = bf16[192,512]{1,0:T(8,128)(2,1)S(1)} fusion(bf16[512,512]{1,0:T(8,128)(2,1)} %param.14, s32[1024]{0:T(1024)S(1)} %pad_clamp_fusion.1), kind=kCustom, calls=%fused_computation | custom fusion | bytes 393984 | tf_op jit(solution)/shard_map/gather | solution.py:794
  11.3 0.0 copy-start.5
  11.3 1.0 gather_fusion.1
  12.3 0.1 add_convert_fusion
  12.5 12.8 %all_gather.3 = bf16[384,1024]{1,0:T(8,128)(2,1)S(1)} all-gather(bf16[192,1024]{1,0:T(8,128)(2,1)S(1)} %pad_maximum_fusion.2), channel_id=1, replica_groups=mesh['row'=4,'col'=2,'seq'=4] {'col'}, dimensions={0}, use_global_device_ids=true | all-gather | bytes 1179648 | tf_op jit(solution)/shard_map/all_gather | solution.py:797
  25.2 0.2 fusion.1
  25.4 1.4 convolution_convert_fusion.2
  26.8 0.0 copy-start.9
  26.8 0.1 reshape.70
  26.9 0.4 convolution_convert_fusion.3
  27.3 0.1 reshape.69
  27.4 0.4 pad_maximum_fusion
  27.8 1.0 copy.20
  28.9 0.9 fusion.7.mask
  29.8 5.8 %convolution_convert_fusion.o_part = bf16[384,4096]{1,0:T(8,128)(2,1)} fusion(bf16[4096,512]{1,0:T(8,128)(2,1)} %param.20, bf16[384,1024]{1,0:T(8,128)(2,1)S(1)} %all_gather.3), kind=kOutput, calls=%fused_computation.2 | convolution fusion | flops 1612185600 | bytes 7733248 | tf_op jit(solution)/shard_map/ld,nd->ln/dot_general | solution.py:818
  35.7 3.5 %convolution_convert_fusion.1.q_part = bf16[384,4096]{1,0:T(8,128)(2,1)} fusion(bf16[512,4096]{1,0:T(8,128)(2,1)S(1)} %copy-done.11, f32[512]{0:T(512)S(1)} %copy-done.8, bf16[384,1024]{1,0:T(8,128)(2,1)S(1)} %all_gather.3), kind=kOutput, calls=%fused_computation.3 | convolution fusion | flops 1612775424 | bytes 7735296 | tf_op jit(solution)/shard_map/dot_general | solution.py:806
  39.1 0.6 broadcast_in_dim.8.sq_part
  39.7 60.0 %shard_map.162 = (f32[384,256]{1,0:T(8,128)}, bf16[384,256]{1,0:T(8,128)(2,1)}, f32[384,256]{1,0:T(8,128)}, f32[8,384]{1,0:T(8,128)}) custom-call(bf16[384,4096]{1,0:T(8,128)(2,1)} %convolution_convert_fusion.1.q_part, bf16[384,4096]{1,0:T(8,128)(2,1)} %convolution_convert_fusion.o_part, bf16[384,1024]{1,0:T(8,128)(2,1)} %bitcast.53, ...), custom_call_target="tpu_custom_call" | custom-call | tf_op jit(solution)/shard_map/pallas_call | solution.py:490
  99.8 0.7 fusion.38
  100.5 0.8 fusion.33
  101.3 0.9 pad_maximum_fusion.3
  102.2 67.2 %shard_map.163 = (bf16[384,4096]{1,0:T(8,128)(2,1)}, bf16[384,4096]{1,0:T(8,128)(2,1)}, bf16[384,1024]{1,0:T(8,128)(2,1)}, f32[8,384]{1,0:T(8,128)}) custom-call(f32[384,256]{1,0:T(8,128)} %get-tuple-element.15.q_sum, bf16[384,256]{1,0:T(8,128)(2,1)} %get-tuple-element.16.o_heads, f32[384,256]{1,0:T(8,128)} %get-tuple-element.17.kv_sum, ...), custom_call_target="tpu_custom_call" | custom-call | tf_op jit(solution)/shard_map/pallas_call | solution.py:744
  169.4 2.1 %reshape.72 = bf16[384,4,256]{2,1,0:T(4,128)(2,1)S(1)} reshape(bf16[384,1024]{1,0:T(8,128)(2,1)} %get-tuple-element.21) | data formatting | bytes 1572864 | tf_op jit(solution)/shard_map/reshape | solution.py:842
  171.5 0.3 fusion.39
  171.9 5.1 %convolution_convert_fusion.4 = bf16[384,512]{1,0:T(8,128)(2,1)S(1)} fusion(bf16[384,4096]{1,0:T(8,128)(2,1)} %get-tuple-element.19, bf16[4096,512]{1,0:T(8,128)(2,1)} %param.20), kind=kOutput, calls=%fused_computation.12 | convolution fusion | flops 1610809344 | bytes 7733248 | tf_op jit(solution)/shard_map/dot_general | solution.py:806
  177.0 0.3 copy-done.12
  177.3 1.8 fusion.40
  179.1 0.4 convolution_add_fusion.1
  179.5 0.5 fusion.3
  180.0 1.0 pad_maximum_fusion.1
  181.0 0.0 reduce-scatter.2.cloned.1.call-update
  181.0 0.7 slice_reduce_fusion
  181.8 4.9 %psum.7 = f32[896]{0:T(1024)S(1)} all-reduce(f32[896]{0:T(1024)S(1)} %pad_maximum_fusion.5), channel_id=1, replica_groups=mesh['row'=4,'col'=2,'seq'=4] {'col'}, use_global_device_ids=true, to_apply=%region_3.0 | all-reduce | flops 896 | bytes 7168 | tf_op jit(solution)/shard_map/psum | solution.py:869
  186.7 0.6 slice.31
  187.3 0.1 constant_dynamic-slice_fusion
  187.4 0.1 multiply_multiply_fusion
  187.4 2.7 %fusion.11 = f32[512,512]{1,0:T(8,128)} fusion(bf16[48,8,4,128]{3,2,1,0:T(4,128)(2,1)} %bitcast.57, f32[384]{0:T(512)S(1)} %get-tuple-element.23, f32[512]{0:T(512)S(1)} %copy-done.8, bf16[384,1024]{1,0:T(8,128)(2,1)S(1)} %all_gather.3), kind=kOutput, calls=%fused_computation.30 | convolution fusion | flops 202113024 | bytes 1839104 | tf_op jit(solution)/shard_map/ld,ln->dn/dot_general | solution.py:851
  190.1 1.5 fusion.14
  191.6 5.8 %fusion.24 = f32[4096,512]{1,0:T(8,128)} fusion(bf16[384,4096]{1,0:T(8,128)(2,1)S(1)} %copy-done.1, bf16[384,1024]{1,0:T(8,128)(2,1)S(1)} %all_gather.3), kind=kOutput, calls=%fused_computation.47 | convolution fusion | flops 1610612736 | bytes 11927552 | tf_op jit(solution)/shard_map/ln,ld->nd/dot_general | solution.py:848
  197.5 5.9 %fusion.36 = f32[512,4096]{1,0:T(8,128)} fusion(bf16[384,4096]{1,0:T(8,128)(2,1)S(1)} %copy-done.3, f32[384]{0:T(512)S(1)} %get-tuple-element.23, f32[512]{0:T(512)S(1)} %copy-done.8, bf16[384,1024]{1,0:T(8,128)(2,1)S(1)} %all_gather.3), kind=kOutput, calls=%fused_computation.69 | convolution fusion | flops 1611399168 | bytes 11931648 | tf_op jit(solution)/shard_map/ld,ln->dn/dot_general | solution.py:849
  203.3 1.1 transpose.23
  204.4 0.1 copy.42
  204.5 0.9 fusion.10
  (31 shorter events, 0.1 us)
Async XLA Ops:
  7.2 4.2 %copy-start = (bf16[1024,512]{1,0:T(8,128)(2,1)S(1)}, bf16[1024,512]{1,0:T(8,128)(2,1)}, u32[]{:S(2)}) copy-start(bf16[1024,512]{1,0:T(8,128)(2,1)} %param.15) | copy-start | bytes 3145732
  7.2 5.2 %copy-start.4 = (bf16[192,512]{1,0:T(8,128)(2,1)S(1)}, bf16[192,512]{1,0:T(8,128)(2,1)}, u32[]{:S(2)}) copy-start(bf16[192,512]{1,0:T(8,128)(2,1)} %param.21) | copy-start | bytes 589828
  7.2 196.2 %reduce-scatter.2.cloned.1.call-start = ((), (), s32[]{:S(2)}) async-start(), calls=%async_computation.1 | async-start | bytes 1179648 | tf_op jit(solution)/shard_map/reduce_scatter | solution.py:859
  9.1 16.2 %copy-start.8 = (f32[512]{0:T(512)S(1)}, f32[512]{0:T(512)}, u32[]{:S(2)}) copy-start(f32[512]{0:T(512)} %param.16) | copy-start | bytes 6148
  11.3 15.6 %copy-start.5 = (bf16[512,512]{1,0:T(8,128)(2,1)S(1)}, bf16[512,512]{1,0:T(8,128)(2,1)}, u32[]{:S(2)}) copy-start(bf16[512,512]{1,0:T(8,128)(2,1)} %param.18) | copy-start | bytes 1572868
  26.8 2.1 copy-start.9
  29.8 5.8 %copy-start.11 = (bf16[512,4096]{1,0:T(8,128)(2,1)S(1)}, bf16[512,4096]{1,0:T(8,128)(2,1)}, u32[]{:S(2)}) copy-start(bf16[512,4096]{1,0:T(8,128)(2,1)} %param.17) | copy-start | bytes 12582916
  39.7 60.8 %copy-start.10 = (f32[64]{0:T(128)S(1)}, f32[64]{0:T(128)}, u32[]{:S(2)}) copy-start(f32[64]{0:T(128)} %multiply_power_fusion) | copy-start | bytes 772
  171.8 7.7 %copy-start.7 = (bf16[384,4,128]{2,1,0:T(4,128)(2,1)}, bf16[384,4,128]{2,1,0:T(4,128)(2,1)S(1)}, u32[]{:S(2)}) copy-start(bf16[384,4,128]{2,1,0:T(4,128)(2,1)S(1)} %get-tuple-element.29) | copy-start | bytes 1179652
  171.8 5.1 %copy-start.2 = (bf16[384,4096]{1,0:T(8,128)(2,1)S(1)}, bf16[384,4096]{1,0:T(8,128)(2,1)}, u32[]{:S(2)}) copy-start(bf16[384,4096]{1,0:T(8,128)(2,1)} %get-tuple-element.20) | copy-start | bytes 9437188
  171.8 5.4 %copy-start.12 = (bf16[512,4096]{1,0:T(8,128)(2,1)S(1)}, bf16[512,4096]{1,0:T(8,128)(2,1)}, u32[]{:S(2)}) copy-start(bf16[512,4096]{1,0:T(8,128)(2,1)} %param.17) | copy-start | bytes 12582916
  177.3 1.8 copy-start.6
  177.3 2.3 %copy-start.13 = (bf16[512,512]{1,0:T(8,128)(2,1)S(1)}, bf16[512,512]{1,0:T(8,128)(2,1)}, u32[]{:S(2)}) copy-start(bf16[512,512]{1,0:T(8,128)(2,1)} %param.19) | copy-start | bytes 1572868
  187.3 4.4 %copy-start.1 = (bf16[384,4096]{1,0:T(8,128)(2,1)S(1)}, bf16[384,4096]{1,0:T(8,128)(2,1)}, u32[]{:S(2)}) copy-start(bf16[384,4096]{1,0:T(8,128)(2,1)} %get-tuple-element.19) | copy-start | bytes 9437188
  191.6 5.8 %copy-start.3 = (bf16[384,4096]{1,0:T(8,128)(2,1)S(1)}, bf16[384,4096]{1,0:T(8,128)(2,1)}, u32[]{:S(2)}) copy-start(bf16[384,4096]{1,0:T(8,128)(2,1)} %get-tuple-element.20) | copy-start | bytes 9437188
Sparse Core Ops, SparseCore 0:
  181.1 17.1 reduce-scatter.1

commit v4 on v3

--- a/solution.py
+++ b/solution.py
@@ -315,13 +315,16 @@
 
 
 def reduce_kernel(
-    q_part, o_part, kv_part, sq_part,
+    q_part, grads, w_hbm, kv_part, sq_part,
     q_out, o_out, kv_out, sq_out,
     q_rc, o_rc, kv_rc, q_a1, o_a1, kv_a1, q_rx, o_rx, kv_rx, q_a2, o_a2, kv_a2,
     q_rz, o_rz, kv_rz, kv_own, kv_all, sq_send, sq_recv,
     core_send, core_recv, x_send, x_recv, z_send, z_recv, kv_send, kv_recv, sq_ss, sq_rs,
+    o_part, w_held, w_sem,
 ):
     f32, bf16 = jnp.float32, jnp.bfloat16
+    w_copy = pltpu.make_async_copy(w_hbm, w_held, w_sem)
+    w_copy.start()
     row, across, core, plane_ids, plane_slots, others, row_ids = neighbours()
     rows = len(others) + 1
     core_id, x_id = plane_ids[0], plane_ids[1]
@@ -361,15 +364,30 @@
                 )
         core_copies.append(copies)
 
-    for index in range(3):
+    for index in range(5):
         start_core(index)
+
+    def output_product():
+        w_copy.wait()
+
+        def tile(step, carry):
+            first = pl.multiple_of(step * wide, wide)
+            o_part[:, pl.ds(first, wide)] = lax.dot_general(
+                grads[...],
+                w_held[pl.ds(first, wide), :],
+                (((1,), (1,)), ((), ())),
+                preferred_element_type=f32,
+            ).astype(bf16)
+            return carry
+
+        lax.fori_loop(0, 2 * rows, tile, 0)
+        for index in range(5, len(pieces)):
+            start_core(index)
 
     def core_stage(index):
         which, b = pieces[index]
         for copy in core_copies[index]:
             copy.wait_recv()
-        if index + 3 < len(pieces):
-            start_core(index + 3)
         if which is None:
             own = kv_part[pl.ds(pl.multiple_of(core * half_len, half_len), half_len), :]
             kv_a1[...] = (own.astype(f32) + kv_rc[...].astype(f32)).astype(bf16)
@@ -442,6 +460,8 @@
     for turn in range(len(pieces) + 5):
         if turn < len(pieces):
             core_stage(turn)
+        if turn == 2:
+            output_product()
         if turn == 1:
             sq_copies[0].wait_recv()
             sq_send[0] = sq_part[...] + sq_recv[0]
@@ -480,7 +500,7 @@
         copy.wait_send()
 
 
-def reduce_shares(q_part, o_part, kv_part, sq_part, rows):
+def reduce_shares(q_part, grads, w_out, kv_part, sq_part, rows):
     f32, bf16 = jnp.float32, jnp.bfloat16
     seq_len, whole = q_part.shape
     width = whole // (4 * rows)
@@ -495,7 +515,13 @@
             jax.ShapeDtypeStruct((seq_len, width), f32),
             jax.ShapeDtypeStruct(sq_part.shape, f32),
         ),
-        in_specs=[pl.BlockSpec(memory_space=pltpu.VMEM)] * 4,
+        in_specs=[
+            pl.BlockSpec(memory_space=pltpu.VMEM),
+            pl.BlockSpec(memory_space=pltpu.VMEM),
+            pl.BlockSpec(memory_space=pl.ANY),
+            pl.BlockSpec(memory_space=pltpu.VMEM),
+            pl.BlockSpec(memory_space=pltpu.VMEM),
+        ],
         out_specs=[pl.BlockSpec(memory_space=pltpu.VMEM)] * 4,
         scratch_shapes=[
             *twice(seq_len, whole // 2),
@@ -515,22 +541,26 @@
             dma((9, rows)), dma((9, rows)), dma((9,)), dma((9,)),
             dma((9, rows - 1)), dma((9, rows - 1)), dma((3,)), dma((3,)),
             dma((1 + rows,)), dma((1 + rows,)),
+            pltpu.VMEM((seq_len, whole), bf16), pltpu.VMEM(w_out.shape, bf16), dma,
         ],
         compiler_params=pltpu.CompilerParams(
             collective_id=0, has_side_effects=True, vmem_limit_bytes=VMEM_BYTES
         ),
-    )(q_part, o_part, kv_part, sq_part)
+    )(q_part, grads, w_out, kv_part, sq_part)
 
 
 def gather_kernel(
-    q_sum, o_heads, kv_sum, squares, mask, cos_ref, sin_ref,
-    a_all, q_all, kv_all, dot_out,
+    q_sum, o_heads, kv_sum, squares, mask, cos_ref, sin_ref, w_hbm,
+    a_all, q_all, kv_all, dot_out, branch,
     a_own, q_own, kv_part, q_heads, probs, tanhs, dot_part,
     kv_recv_buf, dot_send, dot_recv,
     z_send, z_recv, x_send, x_recv, core_send, core_recv,
     r_send, r_recv, kz_send, kz_recv, kp_send, kp_recv, dot_ss, dot_rs,
+    w_held, w_sem,
 ):
     f32, bf16 = jnp.float32, jnp.bfloat16
+    w_copy = pltpu.make_async_copy(w_hbm, w_held, w_sem)
+    w_copy.start()
     row, across, core, plane_ids, plane_slots, others, row_ids = neighbours()
     rows = len(others) + 1
     core_id, x_id = plane_ids[0], plane_ids[1]
@@ -725,9 +755,16 @@
             )
         if turn >= 2:
             core_stage(turn - 2)
+        if turn == 6:
+            w_copy.wait()
+        if 6 <= turn <= 9:
+            for copy in core_copies[turn - 6]:
+                copy.wait_recv()
+            lines = pl.ds((turn - 6) * block, block)
+            branch[lines, :] = dot(a_all[lines, :], w_held[...], (1, 0)).astype(bf16)
     dot_copies[rows].wait_recv()
     dot_out[...] = dot_send[1] + dot_recv[rows]
-    for copy in kv_plane + sum(core_copies, []):
+    for copy in kv_plane + sum(core_copies[4:], []):
         copy.wait_recv()
     for copy in (
         sum(z_copies + x_copies + core_copies, []) + reduces + kv_z + kv_plane + dot_copies
@@ -735,7 +772,7 @@
         copy.wait_send()
 
 
-def attend_and_gather(q_sum, o_heads, kv_sum, squares, mask, cosines, sines, rows):
+def attend_and_gather(q_sum, o_heads, kv_sum, squares, mask, cosines, sines, w_out, rows):
     f32, bf16 = jnp.float32, jnp.bfloat16
     seq_len, width = q_sum.shape
     block = seq_len // 4
@@ -748,9 +785,11 @@
             jax.ShapeDtypeStruct((seq_len, whole), bf16),
             jax.ShapeDtypeStruct((seq_len, rows * width), bf16),
             jax.ShapeDtypeStruct(squares.shape, f32),
+            jax.ShapeDtypeStruct((seq_len, w_out.shape[1]), bf16),
         ),
-        in_specs=[pl.BlockSpec(memory_space=pltpu.VMEM)] * 7,
-        out_specs=[pl.BlockSpec(memory_space=pltpu.VMEM)] * 4,
+        in_specs=[pl.BlockSpec(memory_space=pltpu.VMEM)] * 7
+        + [pl.BlockSpec(memory_space=pl.ANY)],
+        out_specs=[pl.BlockSpec(memory_space=pltpu.VMEM)] * 5,
         scratch_shapes=[
             *[pltpu.VMEM((seq_len, width), bf16)] * 4,
             *[pltpu.VMEM((2, seq_len, seq_len), f32)] * 2,
@@ -762,11 +801,12 @@
             dma((8, rows)), dma((8, rows)), dma((3,)), dma((3,)),
             dma((rows - 1,)), dma((rows - 1,)), dma((3,)), dma((3,)),
             dma((rows + 1,)), dma((rows + 1,)),
+            pltpu.VMEM(w_out.shape, bf16), dma,
         ],
         compiler_params=pltpu.CompilerParams(
             collective_id=1, has_side_effects=True, vmem_limit_bytes=VMEM_BYTES
         ),
-    )(q_sum, o_heads, kv_sum, squares, mask, cosines, sines)
+    )(q_sum, o_heads, kv_sum, squares, mask, cosines, sines, w_out)
 
 
 def fast_device(
@@ -790,15 +830,20 @@
     model_width = out_grad.shape[1]
     kv_width = w_key.shape[1]
 
-    embedded = (
-        motion_table.at[motion_ids].get(mode="promise_in_bounds").astype(f32)
-        + audio_table.at[audio_ids].get(mode="promise_in_bounds").astype(f32)
+    swap = [(0, 1), (1, 0)]
+
+    def both_cols(own, other):
+        return jnp.concatenate(
+            [jnp.where(col_index == 0, own, other), jnp.where(col_index == 0, other, own)], axis=0
+        )
+
+    grad_all = both_cols(out_grad, lax.ppermute(out_grad, "col", swap))
+    ids = jnp.stack([motion_ids, audio_ids], axis=1)
+    ids_all = both_cols(ids, lax.ppermute(ids, "col", swap))
+    embedded_all = (
+        motion_table.at[ids_all[:, 0]].get(mode="promise_in_bounds").astype(f32)
+        + audio_table.at[ids_all[:, 1]].get(mode="promise_in_bounds").astype(f32)
     ).astype(bf16)
-    both = lax.all_gather(
-        jnp.concatenate([embedded, out_grad], axis=1), "col", axis=0, tiled=True
-    )
-    embedded_all = both[:, :model_width]
-    grad_all = both[:, model_width:]
     residual_all = embedded_all.astype(f32)
     scaled = (residual_all * norm_gain[None, :]).astype(bf16)
 
@@ -815,10 +860,10 @@
         ],
         axis=2,
     ).reshape(seq_len, 2 * kv_width)
-    out_part = jnp.einsum("ld,nd->ln", grad_all, w_out, preferred_element_type=f32).astype(bf16)
     query_sum, out_heads, kv_sum, squares = reduce_shares(
         product(scaled, w_query),
-        out_part,
+        grad_all,
+        w_out,
         kv_part,
         as_rows(jnp.sum(residual_all * residual_all, axis=1)),
         row_devices,
@@ -829,7 +874,7 @@
     allowed = (positions[None, :] <= positions[:, None]) & (
         segment_ids[None, :] == segment_ids[:, None]
     )
-    out_all, grad_query_all, kv_grad_all, dot_sum = attend_and_gather(
+    out_all, grad_query_all, kv_grad_all, dot_sum, branch_part = attend_and_gather(
         query_sum,
         out_heads,
         kv_sum,
@@ -837,14 +882,17 @@
         allowed.astype(f32),
         jnp.concatenate([cosines, cosines], axis=1),
         jnp.concatenate([-sines, sines], axis=1),
+        w_out,
         row_devices,
     )
-    kv_grad_all = kv_grad_all.reshape(seq_len, row_devices, 2 * HD)
-    grad_key_all = kv_grad_all[:, :, :HD].reshape(seq_len, kv_width)
-    grad_value_all = kv_grad_all[:, :, HD:].reshape(seq_len, kv_width)
+    grad_key_all, grad_value_all = (
+        jnp.concatenate(
+            [kv_grad_all[:, at : at + HD] for at in range(first, 2 * kv_width, 2 * HD)], axis=1
+        )
+        for first in (0, HD)
+    )
 
     normed = (residual_all * inverse[:, None] * norm_gain[None, :]).astype(bf16)
-    branch_part = product(out_all, w_out)
     grad_wo = jnp.einsum("ln,ld->nd", out_all, grad_all, preferred_element_type=f32)
     grad_wq = jnp.einsum("ld,ln->dn", normed, grad_query_all, preferred_element_type=f32)
     grad_wk = jnp.einsum("ld,ln->dn", normed, grad_key_all, preferred_element_type=f32)
@@ -866,13 +914,14 @@
         .reshape(own_len, 2, model_width)
         .swapaxes(0, 1)
     )
-    sums = lax.psum(jnp.concatenate([gain_part, dot_sum[0]]), "col")
+    sums = jnp.concatenate([gain_part, dot_sum[0]])
+    sums = sums + lax.ppermute(sums, "col", swap)
     grad_gain, dot_sum = sums[:model_width], sums[model_width:]
 
     def own_part(array):
         return lax.dynamic_slice_in_dim(array, col_index * own_len, own_len, axis=0)
 
-    residual = embedded.astype(f32)
+    residual = own_part(residual_all)
     inverse_own = own_part(inverse)[:, None]
     layer_out = (residual + branch_sum).astype(bf16)
     grad_input = (

time: 213 us -> 196 us (0.920)
  blocking collectives: 17.7 us -> 0 us
  matrix products: 34.8 us -> 29.1 us
  starting transfers between devices: 0.04 us -> 4.78 us
  other arithmetic: 8.96 us -> 11.3 us
    all_gather x1 -> x0, blocking collectives: 12.8 us -> none  [fast_device(): lax.all_gather(jnp.concatenate([embedded, out_grad], axis=1), 'col', axis...]
    dot_general x1 -> x0, matrix products: 5.83 us -> none  [fast_device(): jnp.einsum('ld,nd->ln', grad_all, w_out, preferred_element_type=f32)]
    psum x1 -> x0, blocking collectives: 4.95 us -> none  [fast_device(): sums = lax.psum(jnp.concatenate([gain_part, dot_sum[0]]), 'col')]
    ppermute x0 -> x3, starting transfers between devices: none -> 4.74 us  [the longest x1 3.02 us: fast_device(): ids_all = both_cols(ids, lax.ppermute(ids, 'col', swap))]
    dot_general x4 -> x3, matrix products: 10.4 us -> 7.44 us  [product(): return jnp.dot(left, right, preferred_element_type=f32).astype(bf16)]
    dot_general x1, matrix products: 5.81 us -> 8.06 us  [fast_device(): jnp.einsum('ln,ld->nd', out_all, grad_all, preferred_element_type=f32)]
    reshape x1 -> x0, local copies, waits for them, and re-layouts: 2.13 us -> none  [fast_device(): kv_grad_all = kv_grad_all.reshape(seq_len, row_devices, 2 * HD)]
  transfers between devices with their start and end apart: 1 -> 4, of which waited for: 0 -> 1; matrix products, arithmetic and copies ran while one was open for 8% -> 17% of each run, Pallas kernels for 0% -> 0%
where the time goes in v4:
time: 196 us; the launch traced here: 195 us
  Pallas kernels  127 us (65%)
  matrix products  29.1 us (15%)
  between operations  14.3 us (7%)
  other arithmetic  11.3 us (6%)
  local copies, waits for them, and re-layouts  7.61 us (4%)
  starting transfers between devices  4.78 us (2%)
    pallas_call x1, Pallas kernels, attend_and_gather(): pl.pallas_call(gather_kernel, out_shape=(jax.ShapeDtypeStruct((seq_len, w...  67.5 us
    pallas_call x1, Pallas kernels, reduce_shares(): pl.pallas_call(reduce_kernel, out_shape=(jax.ShapeDtypeStruct((seq_len, w...  59.4 us
    dot_general x1, matrix products, fast_device(): jnp.einsum('ln,ld->nd', out_all, grad_all, preferred_element_type=f32)  8.06 us
    dot_general x3, matrix products, product(): return jnp.dot(left, right, preferred_element_type=f32).astype(bf16)  7.44 us
    dot_general x1, matrix products, fast_device(): jnp.einsum('ld,ln->dn', normed, grad_query_all, preferred_element_type=f32)  5.88 us
  transfers between devices with their start and end apart: 4, of which 1 were waited for; matrix products, arithmetic and copies ran while one was open for 17% of the time, Pallas kernels for 0%

profile of v4, /device:TPU:0, one launch (start us, length us, event | category | flops | bytes accessed | tf_op | source)
XLA Modules:
  0.0 195.2 jit_solution(8119223302536322605)
XLA Ops:
  7.2 0.0 copy-start
  7.2 0.0 reduce-scatter.2.cloned.1.call-start
  7.2 0.8 pad_add_fusion
  8.1 3.0 %collective-permute-start = (s32[192,2]{0,1:T(2,128)S(1)}, s32[192,2]{0,1:T(2,128)S(1)}, u32[]{:S(2)}, u32[]{:S(2)}) collective-permute-start(s32[192,2]{0,1:T(2,128)S(1)} %pad_add_fusion), channel_id=1, source_target_pairs={{0,4},{4,0},{1,5},{5,1},{2,6},{6,2},{3,7},{7,3},{8,12},{12,8},{9,1... | collective-permute-start | bytes 4616 | tf_op jit(solution)/shard_map/ppermute | solution.py:842
  11.1 0.1 collective-permute-start.1
  11.2 1.7 fusion.1.mask
  12.9 0.8 fusion.11
  13.6 0.9 pad_maximum_fusion.5
  14.6 0.7 broadcast_select_fusion.3
  15.3 0.1 fusion.12
  15.4 2.1 %gather_fusion.1 = bf16[384,512]{1,0:T(8,128)(2,1)S(1)} fusion(bf16[1024,512]{1,0:T(8,128)(2,1)S(1)} %copy-done, s32[1024]{0:T(1024)S(1)} %get-tuple-element.51), kind=kCustom, calls=%fused_computation.1 | custom fusion | bytes 787968 | tf_op jit(solution)/shard_map/gather | solution.py:845
  17.4 0.0 copy-start.5
  17.5 2.1 %gather_fusion = bf16[384,512]{1,0:T(8,128)(2,1)S(1)} fusion(bf16[512,512]{1,0:T(8,128)(2,1)S(1)} %copy-done.1, s32[1024]{0:T(1024)S(1)} %get-tuple-element.52), kind=kCustom, calls=%fused_computation | custom fusion | bytes 787968 | tf_op jit(solution)/shard_map/gather | solution.py:844
  19.6 0.1 fusion.23
  19.7 0.4 convolution_convert_fusion.2
  20.1 0.1 reshape.60
  20.2 1.4 convolution_convert_fusion.1
  21.6 0.1 reshape.61
  21.7 5.7 %convolution_convert_fusion.q_part = bf16[384,4096]{1,0:T(8,128)(2,1)} fusion(bf16[512,4096]{1,0:T(8,128)(2,1)} %param.17, bf16[384,512]{1,0:T(8,128)(2,1)S(1)} %get-tuple-element.30, f32[512]{0:T(512)S(1)} %copy-done.8), kind=kOutput, calls=%fused_computation.2 | convolution fusion | flops 1612775424 | bytes 7735296 | tf_op jit(solution)/shard_map/dot_general | solution.py:851
  27.4 0.4 pad_maximum_fusion
  27.8 1.0 copy.21
  28.8 0.2 multiply_reduce_fusion.1
  29.0 1.0 broadcast_select_fusion.1
  30.0 0.8 pad_maximum_fusion.2.grads
  30.7 0.6 broadcast_in_dim.2.sq_part
  31.3 59.4 %shard_map.162 = (f32[384,256]{1,0:T(8,128)}, bf16[384,256]{1,0:T(8,128)(2,1)}, f32[384,256]{1,0:T(8,128)}, f32[8,384]{1,0:T(8,128)}) custom-call(bf16[384,4096]{1,0:T(8,128)(2,1)} %convolution_convert_fusion.q_part, bf16[384,512]{1,0:T(8,128)(2,1)} %pad_maximum_fusion.2.grads, bf16[4096,512]{1,0:T(8,128)(2,1)} %w_hbm.3, bf16[384,1024]{1,0:T(8,128)(2,1)} %bitcast.39, ...), custom_call_target="tpu_custom_call" | custom-call | tf_op jit(solution)/shard_map/pallas_call | solution.py:510
  90.7 0.0 copy-start.9
  90.7 0.9 fusion.22
  91.6 67.5 %shard_map.163 = (bf16[384,4096]{1,0:T(8,128)(2,1)}, bf16[384,4096]{1,0:T(8,128)(2,1)}, bf16[384,1024]{1,0:T(8,128)(2,1)}, f32[8,384]{1,0:T(8,128)}, bf16[384,512]{1,0:T(8,128)(2,1)}) custom-call(f32[384,256]{1,0:T(8,128)} %get-tuple-element.16.q_sum, bf16[384,256]{1,0:T(8,128)(2,1)} %get-tuple-element.17.o_heads, f32[384,256]{1,0:T(8,128)} %get-tuple-element.18.kv_sum, ...), custom_call_target="tpu_custom_call" | custom-call | tf_op jit(solution)/shard_map/pallas_call | solution.py:781
  159.1 0.7 slice_reduce_fusion
  159.8 3.8 %fusion.25 = f32[384,512]{1,0:T(8,128)S(1)} fusion(bf16[384,4096]{1,0:T(8,128)(2,1)} %get-tuple-element.21, bf16[512,4096]{1,0:T(8,128)(2,1)S(1)} %copy-done.9), kind=kOutput, calls=%fused_computation.69 | convolution fusion | flops 1610612736 | bytes 8126464 | tf_op jit(solution)/shard_map/ln,dn->ld/dot_general | solution.py:901
  163.6 0.1 fusion.24
  163.8 0.4 convolution_add_fusion.1
  164.2 1.5 fusion.10
  165.8 1.5 fusion.9
  167.3 0.5 multiply_reduce_fusion
  167.8 1.0 pad_maximum_fusion.1
  168.8 0.0 reduce-scatter.2.cloned.1.call-update
  168.8 1.6 collective-permute-start.2
  170.5 8.1 %fusion.20 = f32[4096,512]{1,0:T(8,128)} fusion(bf16[384,4096]{1,0:T(8,128)(2,1)} %get-tuple-element.24, bf16[192,512]{1,0:T(8,128)(2,1)S(1)} %get-tuple-element.44, bf16[192,512]{1,0:T(8,128)(2,1)S(1)} %get-tuple-element.43), kind=kOutput, calls=%fused_computation.64 | convolution fusion | flops 1611399168 | bytes 11927552 | tf_op jit(solution)/shard_map/ln,ld->nd/dot_general | solution.py:896
  178.5 5.9 %fusion.21 = f32[512,4096]{1,0:T(8,128)} fusion(bf16[384,4096]{1,0:T(8,128)(2,1)S(1)} %copy-done.2, bf16[384,512]{1,0:T(8,128)(2,1)S(1)} %get-tuple-element.30, f32[384]{0:T(512)S(1)} %get-tuple-element.27, f32[512]{0:T(512)S(1)} %copy-done.8), kind=kOutput, calls=%fused_computation.65 | convolution fusion | flops 1611399168 | bytes 11931136 | tf_op jit(solution)/shard_map/ld,ln->dn/dot_general | solution.py:897
  184.4 0.1 constant_dynamic-slice_fusion
  184.5 0.6 slice.55
  185.1 0.1 multiply_multiply_fusion
  185.2 1.2 reduce-scatter.2.cloned.1.call-done
  186.3 1.1 transpose.23
  187.4 0.1 copy.23
  187.5 0.9 fusion.6
  (28 shorter events, 0.1 us)
Async XLA Ops:
  7.2 8.2 %copy-start = (bf16[1024,512]{1,0:T(8,128)(2,1)S(1)}, bf16[1024,512]{1,0:T(8,128)(2,1)}, u32[]{:S(2)}) copy-start(bf16[1024,512]{1,0:T(8,128)(2,1)} %param.15) | copy-start | bytes 3145732
  7.2 10.3 %copy-start.1 = (bf16[512,512]{1,0:T(8,128)(2,1)S(1)}, bf16[512,512]{1,0:T(8,128)(2,1)}, u32[]{:S(2)}) copy-start(bf16[512,512]{1,0:T(8,128)(2,1)} %param.14) | copy-start | bytes 1572868
  7.2 179.2 %reduce-scatter.2.cloned.1.call-start = ((), (), s32[]{:S(2)}) async-start(), calls=%async_computation.1 | async-start | bytes 1179648 | tf_op jit(solution)/shard_map/reduce_scatter | solution.py:907
  8.1 6.5 %collective-permute-start = (s32[192,2]{0,1:T(2,128)S(1)}, s32[192,2]{0,1:T(2,128)S(1)}, u32[]{:S(2)}, u32[]{:S(2)}) collective-permute-start(s32[192,2]{0,1:T(2,128)S(1)} %pad_add_fusion), channel_id=1, source_target_pairs={{0,4},{4,0},{1,5},{5,1},{2,6},{6,2},{3,7},{7,3},{8,12},{12,8},{9,1... | collective-permute-start | bytes 4616 | tf_op jit(solution)/shard_map/ppermute | solution.py:842
  11.1 17.9 %collective-permute-start.1 = (bf16[192,512]{1,0:T(8,128)(2,1)}, bf16[192,512]{1,0:T(8,128)(2,1)}, u32[]{:S(2)}, u32[]{:S(2)}) collective-permute-start(bf16[192,512]{1,0:T(8,128)(2,1)} %param.21), channel_id=1, source_target_pairs={{0,4},{4,0},{1,5},{5,1},{2,6},{6,2},{3,7},{7,3},{8,12},{12,8},{9,1... | collective-permute-start | bytes 589832 | tf_op jit(solution)/shard_map/ppermute | solution.py:840
  17.4 2.2 %copy-start.5 = (bf16[512,512]{1,0:T(8,128)(2,1)S(1)}, bf16[512,512]{1,0:T(8,128)(2,1)}, u32[]{:S(2)}) copy-start(bf16[512,512]{1,0:T(8,128)(2,1)} %param.18) | copy-start | bytes 1572868
  17.5 2.2 %copy-start.8 = (f32[512]{0:T(512)S(1)}, f32[512]{0:T(512)}, u32[]{:S(2)}) copy-start(f32[512]{0:T(512)} %param.16) | copy-start | bytes 6148
  27.4 1.6 copy-start.4
  90.7 69.1 %copy-start.9 = (bf16[512,4096]{1,0:T(8,128)(2,1)S(1)}, bf16[512,4096]{1,0:T(8,128)(2,1)}, u32[]{:S(2)}) copy-start(bf16[512,4096]{1,0:T(8,128)(2,1)} %param.17) | copy-start | bytes 12582916
  159.8 3.8 %copy-start.3 = (bf16[384,1024]{1,0:T(8,128)(2,1)S(1)}, bf16[384,1024]{1,0:T(8,128)(2,1)}, u32[]{:S(2)}) copy-start(bf16[384,1024]{1,0:T(8,128)(2,1)} %get-tuple-element.22) | copy-start | bytes 2359300
  159.8 4.0 %copy-start.6 = (bf16[512,512]{1,0:T(8,128)(2,1)S(1)}, bf16[512,512]{1,0:T(8,128)(2,1)}, u32[]{:S(2)}) copy-start(bf16[512,512]{1,0:T(8,128)(2,1)} %param.18) | copy-start | bytes 1572868
  164.2 3.1 %copy-start.10 = (bf16[512,512]{1,0:T(8,128)(2,1)S(1)}, bf16[512,512]{1,0:T(8,128)(2,1)}, u32[]{:S(2)}) copy-start(bf16[512,512]{1,0:T(8,128)(2,1)} %param.19) | copy-start | bytes 1572868
  165.8 2.0 %copy-start.7 = (bf16[384,512]{1,0:T(8,128)(2,1)S(1)}, bf16[384,512]{1,0:T(8,128)(2,1)}, u32[]{:S(2)}) copy-start(bf16[384,512]{1,0:T(8,128)(2,1)} %get-tuple-element.20) | copy-start | bytes 1179652
  168.8 15.7 %collective-permute-start.2 = (f32[896]{0:T(1024)S(1)}, f32[896]{0:T(1024)S(1)}, u32[]{:S(2)}, u32[]{:S(2)}) collective-permute-start(f32[896]{0:T(1024)S(1)} %pad_maximum_fusion.11), channel_id=1, source_target_pairs={{0,4},{4,0},{1,5},{5,1},{2,6},{6,2},{3,7},{7,3},{8,12},{12,8},{9,1... | collective-permute-start | bytes 10760 | tf_op jit(solution)/shard_map/ppermute | solution.py:918
  170.5 8.1 %copy-start.2 = (bf16[384,4096]{1,0:T(8,128)(2,1)S(1)}, bf16[384,4096]{1,0:T(8,128)(2,1)}, u32[]{:S(2)}) copy-start(bf16[384,4096]{1,0:T(8,128)(2,1)} %get-tuple-element.21) | copy-start | bytes 9437188
Sparse Core Ops, SparseCore 0:
  168.9 17.3 reduce-scatter.1
